TPU v7x, 512 devices: a whole 4x8x8 slice. The times are simulated.
512 devices in a mesh: mem: 8 (over z_lo, core), tile: 64 (over x, y, z_hi).
Axes of the slice: x: 4, y: 8, z: 8 (z_hi: 2, z_lo: 4; z = z_hi * 4 + z_lo), core: 2. Of those that a mesh axis runs over, the one named last changes fastest.
Arguments:
- background: bfloat16 [64, 3, 64, 8192], P('mem', None, None, 'tile'), may hold values from -12 to 12
- obs_value: bfloat16 [64, 8192], P('mem', 'tile'), may hold values from -6 to 6
- obs_var: bfloat16 [64, 8192], P('mem', 'tile'), may hold values from 1 to 16
- obs_index: int32 [8, 512, 256], P('mem', 'tile'), may hold values from 0 to 2175
- ice_mask: int32 [64, 8192], P(None, 'tile'), may hold values 0 or 1
- wind_stress: bfloat16 [2, 64, 8192], P(None, None, 'tile'), may hold values from -3 to 3
Outputs:
- forecast: bfloat16 [64, 3, 64, 8192], P('mem', None, None, 'tile')
Inputs may be any that keep to these rules, and one draw needn't show every extreme that they name: Entry k of obs_index[g, p] is the cell r = k // 272, c = k % (272) of the window of row block g and patch p: row g*8+r, column (p*16 - 128+c) mod 8192.
All inputs are finite; a program needn't handle non-finite values. No bound on the sum of `ice_mask` on one device may be relied on, other than what follows from the above.
Results may differ from a plain program's by a relative error of at most 0.0029.
Values may be sent and summed in bfloat16 or wider, within the bound.
A program may use at most 64 MiB of HBM per device.

v0:
```python
import jax
import jax.numpy as jnp
from jax import lax
from jax.sharding import PartitionSpec as P

MEM_DEV = 8
PC = 16
W = 128
NS_ITERS = 6


STRENGTH = 1.0


def extended(cells, sides, width):
    for axis, dim in sides:
        count = lax.axis_size(axis)
        head = lax.slice_in_dim(cells, 0, width, axis=dim)
        tail = lax.slice_in_dim(cells, cells.shape[dim] - width, cells.shape[dim], axis=dim)
        cells = jnp.concatenate(
            [
                lax.ppermute(tail, axis, [(i, (i + 1) % count) for i in range(count)]),
                cells,
                lax.ppermute(head, axis, [((i + 1) % count, i) for i in range(count)]),
            ],
            axis=dim,
        )
    return cells


def for_sending(x):

    def short(part):
        return part.astype(jnp.bfloat16) if part.dtype == jnp.float32 else part

    return jax.tree.map(short, x)


def row_slope(field):
    widths = [(0, 0)] * (field.ndim - 2) + [(1, 1), (0, 0)]
    padded = jnp.pad(field, widths)
    return (padded[..., 2:, :] - padded[..., :-2, :]) * 0.5


def column_slope(field):
    return (field[..., 2:] - field[..., :-2]) * 0.5


def new_stress(drift_x, drift_y, first, second, shear, pressure):
    dxx = column_slope(drift_x)
    dyx = column_slope(drift_y)
    dxy = row_slope(drift_x[..., 1:-1])
    dyy = row_slope(drift_y[..., 1:-1])
    first = (first + pressure * (dxx + dyy) - 0.5 * pressure) * 0.5
    second = (second + 0.25 * pressure * (dxx - dyy)) * 0.5
    shear = (shear + 0.25 * pressure * (dxy + dyx)) * 0.5
    return (first, second, shear)


def new_drift(drift_x, drift_y, first, second, shear, mask, tau_x, tau_y):
    normal_x = 0.5 * (first + second)
    normal_y = 0.5 * (first - second)
    force_x = column_slope(normal_x) + row_slope(shear[..., 1:-1])
    force_y = column_slope(shear) + row_slope(normal_y[..., 1:-1])
    drift_x = mask * (drift_x + 0.5 * (force_x + tau_x)) / 1.5
    drift_y = mask * (drift_y + 0.5 * (force_y + tau_y)) / 1.5
    return (drift_x, drift_y)


def letkf_weights(ens_obs, obs_y, obs_err):
    members = ens_obs.shape[0]
    hp = lax.Precision.HIGHEST
    obs_mean = jnp.mean(ens_obs, axis=0)
    obs_anom = ens_obs - obs_mean
    inverse_var = 1.0 / obs_err
    innovation = obs_y - obs_mean
    identity = jnp.eye(members, dtype=jnp.float32)
    system = jnp.einsum("ipl,jpl->pij", obs_anom * inverse_var, obs_anom, precision=hp)
    system = system + (members - 1.0) * identity
    scale = jnp.sqrt(jnp.sum(system * system, axis=(1, 2)))[:, None, None]
    iterate = system / scale
    inverse_root = jnp.broadcast_to(identity, system.shape)
    for sweep in range(NS_ITERS):
        factor = 1.5 * identity - 0.5 * jnp.einsum(
            "pij,pjk->pik", inverse_root, iterate, precision=hp
        )
        iterate = jnp.einsum("pij,pjk->pik", iterate, factor, precision=hp)
        inverse_root = jnp.einsum("pij,pjk->pik", factor, inverse_root, precision=hp)
    root = inverse_root / jnp.sqrt(scale)
    covariance = jnp.einsum("pij,pjk->pik", root, root, precision=hp)
    projected = jnp.einsum("ipl,pl->pi", obs_anom, inverse_var * innovation, precision=hp)
    mean_weight = jnp.einsum("pij,pj->pi", covariance, projected, precision=hp)
    return jnp.sqrt(members - 1.0) * root + mean_weight[:, :, None]


def patch_weights(thickness, obs_value, obs_var, obs_index):
    members, rows, columns = thickness.shape
    packed = jnp.concatenate([thickness, obs_value[None], obs_var[None]], axis=0)
    lists = obs_index[0]
    patches = lists.shape[0]
    span = PC + 2 * W
    patch_start = (jnp.arange(patches, dtype=jnp.int32) * PC)[:, None]
    window = extended(packed, (("tile", 2),), W)
    wide = columns + 2 * W
    row_of = lists // span
    col_of = lists % span
    flat = row_of * wide + patch_start + col_of
    picked = jnp.take(window.reshape(members + 2, rows * wide), flat.reshape(-1), axis=1)
    picked = picked.reshape(members + 2, patches, lists.shape[1])
    picked = picked.astype(jnp.float32)
    return letkf_weights(picked[:members], picked[members], picked[members + 1])


def body(background, obs_value, obs_var, obs_index, ice_mask, wind_stress):
    hp = lax.Precision.HIGHEST
    groups = lax.axis_size("mem")
    owned = lax.all_to_all(background, "mem", split_axis=2, concat_axis=0, tiled=True)
    weights = patch_weights(owned[:, 0], obs_value, obs_var, obs_index)
    members, fields_count, rows, columns = owned.shape
    patches = columns // PC
    blocks = owned.astype(jnp.float32).reshape(members, fields_count, rows, patches, PC)
    prior_mean = jnp.mean(blocks, axis=0)
    anomalies = blocks - prior_mean
    analysed = prior_mean + jnp.einsum("pij,ivrpc->jvrpc", weights, anomalies, precision=hp)
    analysed = analysed.astype(jnp.bfloat16).reshape(groups, MEM_DEV, fields_count, rows, columns)
    mask = ice_mask.astype(jnp.float32)
    tau = wind_stress.astype(jnp.float32)
    member_fields = lax.all_to_all(analysed, "mem", split_axis=0, concat_axis=3, tiled=True)[0]
    count = member_fields.shape[0]
    fields = member_fields.astype(jnp.float32)
    drift_x = fields[:, 1]
    drift_y = fields[:, 2]
    pressure = STRENGTH * jax.nn.softplus(fields[:, 0])
    first = jnp.zeros_like(pressure)
    second = jnp.zeros_like(pressure)
    shear = jnp.zeros_like(pressure)
    for sweep in range(2):
        wide = extended(for_sending(jnp.concatenate([drift_x, drift_y], axis=0)), (("tile", 2),), 1)
        first, second, shear = new_stress(
            wide[:count], wide[count:], first, second, shear, pressure
        )
        rims = extended(
            for_sending(jnp.concatenate([first, second, shear], axis=0)), (("tile", 2),), 1
        )
        drift_x, drift_y = new_drift(
            drift_x,
            drift_y,
            rims[:count],
            rims[count : 2 * count],
            rims[2 * count :],
            mask,
            tau[0],
            tau[1],
        )
    result = jnp.stack(
        [member_fields[:, 0], drift_x.astype(jnp.bfloat16), drift_y.astype(jnp.bfloat16)], axis=1
    )
    returned = result[None]
    return returned[0]


def solution(mesh):
    placed = (
        P("mem", None, None, "tile"),
        P("mem", "tile"),
        P("mem", "tile"),
        P("mem", "tile", None),
        P(None, "tile"),
        P(None, None, "tile"),
    )
    return jax.shard_map(
        body, mesh=mesh, in_specs=placed, out_specs=P("mem", None, None, "tile"), check_vma=False
    )
```

profile of v0, /device:TPU:4, one launch (start us, length us, event | category | flops | bytes accessed | tf_op | source)
XLA Modules:
  0.0 249.8 jit_solution(2959730376562601100)
XLA Ops:
  0.0 2.0 copy.50
  2.0 7.3 %all-to-all-start = ((bf16[8,3,64,128]{3,0,1,2:T(8,128)(2,1)}), bf16[8,3,64,128]{3,0,1,2:T(8,128)(2,1)S(1)}, u32[]{:S(2)}, u32[]{:S(2)}) async-start(bf16[8,3,64,128]{3,0,1,2:T(8,128)(2,1)} %copy.50), calls=%async_computation | async-start | bytes 786432 | tf_op jit(solution)/shard_map/all_to_all | solution.py:117
  9.7 12.2 %all-to-all-done = bf16[8,3,64,128]{3,0,1,2:T(8,128)(2,1)S(1)} async-done(((bf16[8,3,64,128]{3,0,1,2:T(8,128)(2,1)}), bf16[8,3,64,128]{3,0,1,2:T(8,128)(2,1)S(1)}, u32[]{:S(2)}, u32[]{:S(2)}) %all-to-all-start) | async-done | bytes 393248 | tf_op jit(solution)/shard_map/all_to_all | solution.py:117
  22.0 11.1 %collective-permute-start.1 = (bf16[66,8,128]{2,1,0:T(8,128)(2,1)S(1)}, bf16[66,8,128]{2,1,0:T(8,128)(2,1)S(1)}, u32[]{:S(2)}, u32[]{:S(2)}) collective-permute-start(bf16[66,8,128]{2,1,0:T(8,128)(2,1)S(1)} %pad_maximum_fusion.16), channel_id=1, source_target_pairs={{1,0},{2,1},{3,2},{4,3},{5,4},{6,5},{7,6},{8,7},{9,8},{10,9},{11,1... | collective-permute-start | bytes 405512 | tf_op jit(solution)/shard_map/ppermute | solution.py:24
  35.2 3.9 %reshape.165 = f32[64,3,8,8,16]{4,3,2,1,0:T(8,128)} reshape(f32[8,8,3,8,128]{4,3,2,1,0:T(8,128)S(1)} %copy.53) | data formatting | bytes 1572864 | tf_op jit(solution)/shard_map/convert_element_type | solution.py:121
  39.1 5.2 %copy.54 = f32[64,3,8,8,16]{0,4,2,1,3:T(8,128)S(1)} copy(f32[64,3,8,8,16]{4,3,2,1,0:T(8,128)} %reshape.165) | data formatting | bytes 1572864 | tf_op jit(solution)/shard_map/convert_element_type | solution.py:121
  44.5 3.8 %collective-permute-done = bf16[66,8,128]{2,1,0:T(8,128)(2,1)S(1)} collective-permute-done((bf16[66,8,128]{2,1,0:T(8,128)(2,1)S(1)}, bf16[66,8,128]{2,1,0:T(8,128)(2,1)S(1)}, u32[]{:S(2)}, u32[]{:S(2)}) %collective-permute-start) | collective-permute-done | bytes 135200 | tf_op jit(solution)/shard_map/ppermute | solution.py:22
  48.9 6.2 %gather_fusion = bf16[2048,66]{1,0:T(8,128)(2,1)S(1)} fusion(bf16[66,3072]{0,1:T(8,128)(2,1)S(1)} %bitcast.176, s32[2048]{0:T(1024)S(1)} %broadcast_clamp_fusion), kind=kCustom, calls=%fused_computation | custom fusion | bytes 548864 | tf_op jit(solution)/shard_map/jit(_take)/gather | solution.py:108
  64.6 2.7 %fusion = bf16[64,3,8,8,16]{0,4,2,1,3:T(8,128)(2,1)} fusion(f32[64,3,8,8,16]{0,4,2,1,3:T(8,128)S(1)} %copy.54, f32[3,8,8,16]{3,1,0,2:T(8,128)S(1)} %copy.52, f32[8,64,64]{2,1,0:T(8,128)S(1)} %convolution_divide_fusion, f32[8,64]{1,0:T(8,128)S(1)} %bitcast.185), kind=kOutput, calls=%fused_computation.2 | convolution fusion | flops 151650304 | bytes 1325056 | tf_op jit(solution)/shard_map/pij,ivrpc->jvrpc/dot_general | solution.py:124
  67.2 5.7 %copy.59 = bf16[64,3,8,8,16]{4,3,2,1,0:T(8,128)(2,1)S(1)} copy(bf16[64,3,8,8,16]{0,4,2,1,3:T(8,128)(2,1)} %fusion) | data formatting | bytes 786432 | tf_op jit(solution)/shard_map/convert_element_type | solution.py:125
  73.0 2.1 reshape.164
  75.1 15.9 %all_to_all.33 = bf16[8,8,3,8,128]{4,3,2,1,0:T(8,128)(2,1)S(1)} all-to-all(bf16[8,8,3,8,128]{4,3,2,1,0:T(8,128)(2,1)S(1)} %reshape.164), channel_id=1, replica_groups=mesh['mem'=8,'tile'=64] {'mem'}, dimensions={0} | all-to-all | bytes 786432 | tf_op jit(solution)/shard_map/all_to_all | solution.py:128
  93.2 10.8 %collective-permute-start.2 = (bf16[16,64,1]{2,1,0:T(8,128)(2,1)S(1)}, bf16[16,64,1]{2,1,0:T(8,128)(2,1)S(1)}, u32[]{:S(2)}, u32[]{:S(2)}) collective-permute-start(bf16[16,64,1]{2,1,0:T(8,128)(2,1)S(1)} %get-tuple-element.39), channel_id=1, source_target_pairs={{1,0},{2,1},{3,2},{4,3},{5,4},{6,5},{7,6},{8,7},{9,8},{10,9},{11,1... | collective-permute-start | bytes 6152 | tf_op jit(solution)/shard_map/ppermute | solution.py:24
  104.1 11.3 %collective-permute-done.3 = bf16[16,64,1]{2,1,0:T(8,128)(2,1)S(1)} collective-permute-done((bf16[16,64,1]{2,1,0:T(8,128)(2,1)S(1)}, bf16[16,64,1]{2,1,0:T(8,128)(2,1)S(1)}, u32[]{:S(2)}, u32[]{:S(2)}) %collective-permute-start.3) | collective-permute-done | bytes 2080 | tf_op jit(solution)/shard_map/ppermute | solution.py:22
  115.4 6.6 %collective-permute-done.2 = bf16[16,64,1]{2,1,0:T(8,128)(2,1)S(1)} collective-permute-done((bf16[16,64,1]{2,1,0:T(8,128)(2,1)S(1)}, bf16[16,64,1]{2,1,0:T(8,128)(2,1)S(1)}, u32[]{:S(2)}, u32[]{:S(2)}) %collective-permute-start.2) | collective-permute-done | bytes 2080 | tf_op jit(solution)/shard_map/ppermute | solution.py:24
  123.3 4.8 %collective-permute-start.5 = (bf16[24,64,1]{2,1,0:T(8,128)(2,1)S(1)}, bf16[24,64,1]{2,1,0:T(8,128)(2,1)S(1)}, u32[]{:S(2)}, u32[]{:S(2)}) collective-permute-start(bf16[24,64,1]{2,1,0:T(8,128)(2,1)S(1)} %get-tuple-element.36), channel_id=1, source_target_pairs={{1,0},{2,1},{3,2},{4,3},{5,4},{6,5},{7,6},{8,7},{9,8},{10,9},{11,1... | collective-permute-start | bytes 9224 | tf_op jit(solution)/shard_map/ppermute | solution.py:24
  128.1 4.9 %collective-permute-start.4 = (bf16[24,64,1]{2,1,0:T(8,128)(2,1)S(1)}, bf16[24,64,1]{2,1,0:T(8,128)(2,1)S(1)}, u32[]{:S(2)}, u32[]{:S(2)}) collective-permute-start(bf16[24,64,1]{2,1,0:T(8,128)(2,1)S(1)} %get-tuple-element.35), channel_id=1, source_target_pairs={{0,1},{1,2},{2,3},{3,4},{4,5},{5,6},{6,7},{7,8},{8,9},{9,10},{10,1... | collective-permute-start | bytes 9224 | tf_op jit(solution)/shard_map/ppermute | solution.py:22
  133.1 28.6 %collective-permute-done.5 = bf16[24,64,1]{2,1,0:T(8,128)(2,1)S(1)} collective-permute-done((bf16[24,64,1]{2,1,0:T(8,128)(2,1)S(1)}, bf16[24,64,1]{2,1,0:T(8,128)(2,1)S(1)}, u32[]{:S(2)}, u32[]{:S(2)}) %collective-permute-start.5) | collective-permute-done | bytes 3104 | tf_op jit(solution)/shard_map/ppermute | solution.py:24
  162.9 4.5 %collective-permute-start.7 = (bf16[16,64,1]{2,1,0:T(8,128)(2,1)S(1)}, bf16[16,64,1]{2,1,0:T(8,128)(2,1)S(1)}, u32[]{:S(2)}, u32[]{:S(2)}) collective-permute-start(bf16[16,64,1]{2,1,0:T(8,128)(2,1)S(1)} %get-tuple-element.38), channel_id=1, source_target_pairs={{0,1},{1,2},{2,3},{3,4},{4,5},{5,6},{6,7},{7,8},{8,9},{9,10},{10,1... | collective-permute-start | bytes 6152 | tf_op jit(solution)/shard_map/ppermute | solution.py:22
  167.4 8.2 %collective-permute-start.6 = (bf16[16,64,1]{2,1,0:T(8,128)(2,1)S(1)}, bf16[16,64,1]{2,1,0:T(8,128)(2,1)S(1)}, u32[]{:S(2)}, u32[]{:S(2)}) collective-permute-start(bf16[16,64,1]{2,1,0:T(8,128)(2,1)S(1)} %get-tuple-element.37), channel_id=1, source_target_pairs={{1,0},{2,1},{3,2},{4,3},{5,4},{6,5},{7,6},{8,7},{9,8},{10,9},{11,1... | collective-permute-start | bytes 6152 | tf_op jit(solution)/shard_map/ppermute | solution.py:24
  175.6 13.6 %collective-permute-done.7 = bf16[16,64,1]{2,1,0:T(8,128)(2,1)S(1)} collective-permute-done((bf16[16,64,1]{2,1,0:T(8,128)(2,1)S(1)}, bf16[16,64,1]{2,1,0:T(8,128)(2,1)S(1)}, u32[]{:S(2)}, u32[]{:S(2)}) %collective-permute-start.7) | collective-permute-done | bytes 2080 | tf_op jit(solution)/shard_map/ppermute | solution.py:22
  192.1 36.4 %collective-permute-start.9 = (bf16[24,64,1]{2,1,0:T(8,128)(2,1)S(1)}, bf16[24,64,1]{2,1,0:T(8,128)(2,1)S(1)}, u32[]{:S(2)}, u32[]{:S(2)}) collective-permute-start(bf16[24,64,1]{2,1,0:T(8,128)(2,1)S(1)} %get-tuple-element.34), channel_id=1, source_target_pairs={{1,0},{2,1},{3,2},{4,3},{5,4},{6,5},{7,6},{8,7},{9,8},{10,9},{11,1... | collective-permute-start | bytes 9224 | tf_op jit(solution)/shard_map/ppermute | solution.py:24
  230.4 6.5 %collective-permute-done.9 = bf16[24,64,1]{2,1,0:T(8,128)(2,1)S(1)} collective-permute-done((bf16[24,64,1]{2,1,0:T(8,128)(2,1)S(1)}, bf16[24,64,1]{2,1,0:T(8,128)(2,1)S(1)}, u32[]{:S(2)}, u32[]{:S(2)}) %collective-permute-start.9) | collective-permute-done | bytes 3104 | tf_op jit(solution)/shard_map/ppermute | solution.py:24
  236.9 11.0 %collective-permute-done.8 = bf16[24,64,1]{2,1,0:T(8,128)(2,1)S(1)} collective-permute-done((bf16[24,64,1]{2,1,0:T(8,128)(2,1)S(1)}, bf16[24,64,1]{2,1,0:T(8,128)(2,1)S(1)}, u32[]{:S(2)}, u32[]{:S(2)}) %collective-permute-start.8) | collective-permute-done | bytes 3104 | tf_op jit(solution)/shard_map/ppermute | solution.py:22
  (93 shorter events, 23.6 us)
Async XLA Ops:
  0.0 9.3 %copy-start = (s32[1,8,256]{2,1,0:T(8,128)S(1)}, s32[1,8,256]{2,1,0:T(8,128)}, u32[]{:S(2)}) copy-start(s32[1,8,256]{2,1,0:T(8,128)} %param.9) | copy-start | bytes 24580
  0.0 21.9 %copy-start.3 = (bf16[8,128]{1,0:T(8,128)(2,1)S(1)}, bf16[8,128]{1,0:T(8,128)(2,1)}, u32[]{:S(2)}) copy-start(bf16[8,128]{1,0:T(8,128)(2,1)} %param.8) | copy-start | bytes 6148
  0.0 21.9 %copy-start.4 = (bf16[8,128]{1,0:T(8,128)(2,1)S(1)}, bf16[8,128]{1,0:T(8,128)(2,1)}, u32[]{:S(2)}) copy-start(bf16[8,128]{1,0:T(8,128)(2,1)} %param.7) | copy-start | bytes 6148
  2.0 19.8 %all-to-all-start = ((bf16[8,3,64,128]{3,0,1,2:T(8,128)(2,1)}), bf16[8,3,64,128]{3,0,1,2:T(8,128)(2,1)S(1)}, u32[]{:S(2)}, u32[]{:S(2)}) async-start(bf16[8,3,64,128]{3,0,1,2:T(8,128)(2,1)} %copy.50), calls=%async_computation | async-start | bytes 786432 | tf_op jit(solution)/shard_map/all_to_all | solution.py:117
  22.0 22.5 %collective-permute-start.1 = (bf16[66,8,128]{2,1,0:T(8,128)(2,1)S(1)}, bf16[66,8,128]{2,1,0:T(8,128)(2,1)S(1)}, u32[]{:S(2)}, u32[]{:S(2)}) collective-permute-start(bf16[66,8,128]{2,1,0:T(8,128)(2,1)S(1)} %pad_maximum_fusion.16), channel_id=1, source_target_pairs={{1,0},{2,1},{3,2},{4,3},{5,4},{6,5},{7,6},{8,7},{9,8},{10,9},{11,1... | collective-permute-start | bytes 405512 | tf_op jit(solution)/shard_map/ppermute | solution.py:24
  33.1 15.2 %collective-permute-start = (bf16[66,8,128]{2,1,0:T(8,128)(2,1)S(1)}, bf16[66,8,128]{2,1,0:T(8,128)(2,1)S(1)}, u32[]{:S(2)}, u32[]{:S(2)}) collective-permute-start(bf16[66,8,128]{2,1,0:T(8,128)(2,1)S(1)} %pad_maximum_fusion.16), channel_id=1, source_target_pairs={{0,1},{1,2},{2,3},{3,4},{4,5},{5,6},{6,7},{7,8},{8,9},{9,10},{10,1... | collective-permute-start | bytes 405512 | tf_op jit(solution)/shard_map/ppermute | solution.py:22
  91.0 13.1 %copy-start.1 = (bf16[2,64,128]{2,1,0:T(8,128)(2,1)S(1)}, bf16[2,64,128]{2,1,0:T(8,128)(2,1)}, u32[]{:S(2)}) copy-start(bf16[2,64,128]{2,1,0:T(8,128)(2,1)} %param.11) | copy-start | bytes 98308
  91.3 24.1 %collective-permute-start.3 = (bf16[16,64,1]{2,1,0:T(8,128)(2,1)S(1)}, bf16[16,64,1]{2,1,0:T(8,128)(2,1)S(1)}, u32[]{:S(2)}, u32[]{:S(2)}) collective-permute-start(bf16[16,64,1]{2,1,0:T(8,128)(2,1)S(1)} %get-tuple-element.40), channel_id=1, source_target_pairs={{0,1},{1,2},{2,3},{3,4},{4,5},{5,6},{6,7},{7,8},{8,9},{9,10},{10,1... | collective-permute-start | bytes 6152 | tf_op jit(solution)/shard_map/ppermute | solution.py:22
  93.2 28.9 %collective-permute-start.2 = (bf16[16,64,1]{2,1,0:T(8,128)(2,1)S(1)}, bf16[16,64,1]{2,1,0:T(8,128)(2,1)S(1)}, u32[]{:S(2)}, u32[]{:S(2)}) collective-permute-start(bf16[16,64,1]{2,1,0:T(8,128)(2,1)S(1)} %get-tuple-element.39), channel_id=1, source_target_pairs={{1,0},{2,1},{3,2},{4,3},{5,4},{6,5},{7,6},{8,7},{9,8},{10,9},{11,1... | collective-permute-start | bytes 6152 | tf_op jit(solution)/shard_map/ppermute | solution.py:24
  122.8 10.3 %copy-start.2 = (s32[64,128]{1,0:T(8,128)S(1)}, s32[64,128]{1,0:T(8,128)}, u32[]{:S(2)}) copy-start(s32[64,128]{1,0:T(8,128)} %param.10) | copy-start | bytes 98308
  123.3 38.4 %collective-permute-start.5 = (bf16[24,64,1]{2,1,0:T(8,128)(2,1)S(1)}, bf16[24,64,1]{2,1,0:T(8,128)(2,1)S(1)}, u32[]{:S(2)}, u32[]{:S(2)}) collective-permute-start(bf16[24,64,1]{2,1,0:T(8,128)(2,1)S(1)} %get-tuple-element.36), channel_id=1, source_target_pairs={{1,0},{2,1},{3,2},{4,3},{5,4},{6,5},{7,6},{8,7},{9,8},{10,9},{11,1... | collective-permute-start | bytes 9224 | tf_op jit(solution)/shard_map/ppermute | solution.py:24
  128.1 33.6 %collective-permute-start.4 = (bf16[24,64,1]{2,1,0:T(8,128)(2,1)S(1)}, bf16[24,64,1]{2,1,0:T(8,128)(2,1)S(1)}, u32[]{:S(2)}, u32[]{:S(2)}) collective-permute-start(bf16[24,64,1]{2,1,0:T(8,128)(2,1)S(1)} %get-tuple-element.35), channel_id=1, source_target_pairs={{0,1},{1,2},{2,3},{3,4},{4,5},{5,6},{6,7},{7,8},{8,9},{9,10},{10,1... | collective-permute-start | bytes 9224 | tf_op jit(solution)/shard_map/ppermute | solution.py:22
  162.9 26.4 %collective-permute-start.7 = (bf16[16,64,1]{2,1,0:T(8,128)(2,1)S(1)}, bf16[16,64,1]{2,1,0:T(8,128)(2,1)S(1)}, u32[]{:S(2)}, u32[]{:S(2)}) collective-permute-start(bf16[16,64,1]{2,1,0:T(8,128)(2,1)S(1)} %get-tuple-element.38), channel_id=1, source_target_pairs={{0,1},{1,2},{2,3},{3,4},{4,5},{5,6},{6,7},{7,8},{8,9},{9,10},{10,1... | collective-permute-start | bytes 6152 | tf_op jit(solution)/shard_map/ppermute | solution.py:22
  167.4 23.3 %collective-permute-start.6 = (bf16[16,64,1]{2,1,0:T(8,128)(2,1)S(1)}, bf16[16,64,1]{2,1,0:T(8,128)(2,1)S(1)}, u32[]{:S(2)}, u32[]{:S(2)}) collective-permute-start(bf16[16,64,1]{2,1,0:T(8,128)(2,1)S(1)} %get-tuple-element.37), channel_id=1, source_target_pairs={{1,0},{2,1},{3,2},{4,3},{5,4},{6,5},{7,6},{8,7},{9,8},{10,9},{11,1... | collective-permute-start | bytes 6152 | tf_op jit(solution)/shard_map/ppermute | solution.py:24
  192.1 44.9 %collective-permute-start.9 = (bf16[24,64,1]{2,1,0:T(8,128)(2,1)S(1)}, bf16[24,64,1]{2,1,0:T(8,128)(2,1)S(1)}, u32[]{:S(2)}, u32[]{:S(2)}) collective-permute-start(bf16[24,64,1]{2,1,0:T(8,128)(2,1)S(1)} %get-tuple-element.34), channel_id=1, source_target_pairs={{1,0},{2,1},{3,2},{4,3},{5,4},{6,5},{7,6},{8,7},{9,8},{10,9},{11,1... | collective-permute-start | bytes 9224 | tf_op jit(solution)/shard_map/ppermute | solution.py:24
  228.5 19.5 %collective-permute-start.8 = (bf16[24,64,1]{2,1,0:T(8,128)(2,1)S(1)}, bf16[24,64,1]{2,1,0:T(8,128)(2,1)S(1)}, u32[]{:S(2)}, u32[]{:S(2)}) collective-permute-start(bf16[24,64,1]{2,1,0:T(8,128)(2,1)S(1)} %get-tuple-element.33), channel_id=1, source_target_pairs={{0,1},{1,2},{2,3},{3,4},{4,5},{5,6},{6,7},{7,8},{8,9},{9,10},{10,1... | collective-permute-start | bytes 9224 | tf_op jit(solution)/shard_map/ppermute | solution.py:22
where the time goes:
time: 250 us
  waiting for transfers between devices  95.2 us (38%)
  starting transfers between devices  93.9 us (38%)
  local copies, waits for them, and re-layouts  27.6 us (11%)
  blocking collectives  15.9 us (6%)
  matrix products  11.6 us (5%)
  other arithmetic  5.06 us (2%)
    ppermute x5, starting transfers between devices, extended(): lax.ppermute(head, axis, [((i + 1) % count, i) for i in range(count)])  71.4 us
    ppermute x5, waiting for transfers between devices, extended(): lax.ppermute(head, axis, [((i + 1) % count, i) for i in range(count)])  43.2 us
    ppermute x5, waiting for transfers between devices, extended(): lax.ppermute(tail, axis, [(i, (i + 1) % count) for i in range(count)])  39.8 us
    all_to_all x1, blocking collectives, body(): lax.all_to_all(analysed, 'mem', split_axis=0, concat_axis=3, tiled=True)[0]  15.9 us
    ppermute x5, starting transfers between devices, extended(): lax.ppermute(tail, axis, [(i, (i + 1) % count) for i in range(count)])  15.2 us
    all_to_all x1, waiting for transfers between devices, body(): lax.all_to_all(background, 'mem', split_axis=2, concat_axis=0, tiled=True)  12.2 us
    convert_element_type x3, local copies, waits for them, and re-layouts, body(): owned.astype(jnp.float32).reshape(members, fields_count, rows, patches, PC)  9.19 us
    all_to_all x1, starting transfers between devices, body(): lax.all_to_all(background, 'mem', split_axis=2, concat_axis=0, tiled=True)  7.27 us
  transfers between devices with their start and end apart: 11, of which 9 were waited for; matrix products, arithmetic and copies ran while one was open for 4% of the time, Pallas kernels for 0%

commit v1 on v0

v1 whole, which is shorter than its diff:
```python
import functools

import jax
import jax.numpy as jnp
from jax import lax
from jax.experimental import pallas as pl
from jax.experimental.pallas import tpu as pltpu
from jax.sharding import PartitionSpec as P

F32 = jnp.float32
BF16 = jnp.bfloat16
MESH = pl.DeviceIdType.MESH

ENS = 64
GROUPS = 8
RB = 8
ROWS = 64
PC = 16
W = 128
SPAN = PC + 2 * W
LANES = 128
PATCHES = 8
FIELDS = 3
NS_ITERS = 6
WIDE = PATCHES * ENS
CELLS = 3 * RB * LANES
HALO = 4


def iota(shape, axis):
    return lax.broadcasted_iota(jnp.int32, shape, axis)


def aligned(start, size, by):
    return pl.ds(pl.multiple_of(start, by), size)


def split(x):
    high = x.astype(BF16)
    return high, (x - high.astype(F32)).astype(BF16)


def dot(a, b):
    return jnp.dot(a, b, preferred_element_type=F32)


def dot_lanes(a, b):
    return lax.dot_general(a, b, (((1,), (1,)), ((), ())), preferred_element_type=F32)


def block_diagonal(x):
    segment = iota(x.shape, 1) // ENS
    zero = jnp.zeros_like(x)
    return jnp.concatenate([jnp.where(segment == q, x, zero) for q in range(4)], axis=0)


def patch_products(left, right):
    rows = left.shape[0]
    left_high, left_low = split(left)
    right_high, right_low = split(right)
    out = []
    for half in range(2):
        lanes = slice(half * 256, (half + 1) * 256)
        both = jnp.concatenate([left_high[:, lanes], left_low[:, lanes]], axis=0)
        main = dot(both, block_diagonal(right_high[:, lanes]))
        rest = dot(left_high[:, lanes], block_diagonal(right_low[:, lanes]))
        out.append(main[:rows] + main[rows:] + rest)
    return jnp.concatenate(out, axis=1)


def root_weights(system, projected):
    row = iota((ENS, WIDE), 0)
    eye = ((iota((ENS, WIDE), 1) % ENS) == row).astype(F32)
    full = system + (ENS - 1.0) * eye
    squares = jnp.sum(full * full, axis=0, keepdims=True)
    own = ((iota((PATCHES, WIDE), 1) // ENS) == iota((PATCHES, WIDE), 0)).astype(F32)
    norm = jnp.sum(own * squares, axis=1, keepdims=True)
    scale = jnp.sqrt(jnp.sum(own * norm, axis=0, keepdims=True))
    centring = eye - 1.0 / ENS
    iterate = (system + (ENS - 1.0) * centring) / scale
    factor = 1.5 * eye - 0.5 * iterate
    inverse_root = 1.5 * centring - 0.5 * iterate
    moved = patch_products(jnp.concatenate([iterate, projected], axis=0), factor)
    iterate, projected = moved[:ENS], moved[ENS:]
    for sweep in range(1, NS_ITERS):
        factor = 1.5 * eye - 0.5 * patch_products(inverse_root, iterate)
        if sweep < NS_ITERS - 1:
            moved = patch_products(jnp.concatenate([iterate, inverse_root, projected], axis=0), factor)
            iterate, inverse_root, projected = moved[:ENS], moved[ENS : 2 * ENS], moved[2 * ENS :]
        else:
            moved = patch_products(jnp.concatenate([inverse_root, projected], axis=0), factor)
            inverse_root, projected = moved[:ENS], moved[ENS:]
    mean_weight = patch_products(projected, inverse_root)[:1] / scale
    return jnp.sqrt(ENS - 1.0) * (inverse_root / jnp.sqrt(scale)) + (mean_weight + 1.0 / ENS)


def kernel(
    tiles,
    bg, obs_value, obs_var, obs_index, ice_mask, wind,
    out,
    turned, send_a, send_obs, thick, drift, obs, index,
    count, weight, anom_hi, anom_lo, heavy_hi, heavy_lo, acc,
    masked, packed, edge_send, edge_recv,
    send_c, recv_c, send_e, recv_e,
    send_w, recv_w,
    mask_f, tau_x, tau_y, press, field_x, field_y, normal_x, normal_y, shear, final,
    at_s, at_r, ad_s, ad_r, ob_s, ob_r, b_s, b_r, n_s, n_r, c_s, c_r, e_s, e_r, w_s, w_r,
):
    me, tile = lax.axis_index("mem"), lax.axis_index("tile")
    core, z_lo = me % 2, me // 2
    half, ring = tile % 2, tile // 2
    z = half * 4 + z_lo

    def ring_device(at_z, at_core):
        return ((at_z % 4) * 2 + at_core, ring * 2 + at_z // 4)

    chip_mate = (me + 1 - 2 * core, tile)
    side_mate = (me + 1 - 2 * core, lax.rem(tile + tiles - 2 + 4 * core, tiles))
    left_tile = lax.rem(tile + tiles - 1, tiles)
    right_tile = lax.rem(tile + 1, tiles)
    outer_tile = jnp.where(half == 0, left_tile, right_tile)

    barrier = pltpu.get_barrier_semaphore()

    def greet(step, carry):
        at = lax.rem(z * 2 + core + step, 16)
        pl.semaphore_signal(barrier, inc=1, device_id=ring_device(at // 2, at % 2), device_id_type=MESH)
        return carry

    lax.fori_loop(1, 16, greet, 0)
    pl.semaphore_signal(barrier, inc=1, device_id=side_mate, device_id_type=MESH)
    pl.semaphore_signal(barrier, inc=1, device_id=(me, outer_tile), device_id_type=MESH)

    def turn(v):
        turned[...] = bg[:, v].astype(F32).reshape(GROUPS * ROWS, LANES)
        for g in range(GROUPS):
            for pair in range(RB // 2):
                parts = [turned[pl.ds(g * RB + pair * 2 + h, 8, stride=ROWS), :] for h in range(2)]
                send_a[g, v, pair * 16 : pair * 16 + 16, :] = jnp.concatenate(parts, axis=0).astype(BF16)

    turn(0)
    send_obs[...] = jnp.concatenate([obs_value[...].astype(F32), obs_var[...].astype(F32)], axis=0).astype(BF16)

    lane = iota((RB, LANES), 1)

    def flat_field(f):
        return ice_mask[...].astype(F32) if f == 0 else wind[f - 1].astype(F32)

    low = jnp.zeros((RB, LANES), F32)
    high = jnp.zeros((RB, LANES), F32)
    for f in range(FIELDS):
        whole = flat_field(f)
        for g in range(GROUPS):
            j = f * GROUPS + g
            rows = whole[g * RB : (g + 1) * RB]
            here = (lane // HALO) == j
            low = jnp.where(here, pltpu.roll(rows, (HALO * j) % LANES, 1), low)
            high = jnp.where(here, pltpu.roll(rows, (HALO * j + HALO) % LANES, 1), high)
    send_w[0] = low
    send_w[1] = high

    pl.semaphore_wait(barrier, 17)

    def remote(src, dst, s_sem, r_sem, device):
        return pltpu.make_async_remote_copy(
            src_ref=src, dst_ref=dst, send_sem=s_sem, recv_sem=r_sem, device_id=device, device_id_type=MESH
        )

    def settle(ref, sem):
        pltpu.make_async_copy(ref, ref, sem).wait()

    def send_or_keep(same, src, dst, s_sem, r_sem, device):
        @pl.when(same)
        def _():
            pltpu.make_async_copy(src, dst, r_sem).start()

        @pl.when(jnp.logical_not(same))
        def _():
            remote(src, dst, s_sem, r_sem, device).start()

    def wait_sent(same, src, s_sem):
        @pl.when(jnp.logical_not(same))
        def _():
            settle(src, s_sem)

    at_home = core == half
    for step in (4, 3, 5, 2, 6, 1, 7, 0):
        g = lax.rem(z + step, GROUPS)
        there = ring_device(g, half)
        if step:
            remote(send_a.at[g, 0], thick.at[1, me], at_s.at[step], at_r.at[me], there).start()
        else:
            send_or_keep(at_home, send_a.at[g, 0], thick.at[1, me], at_s.at[step], at_r.at[me], there)
    owner = ring_device(me, half)
    obs_home = jnp.logical_and(owner[0] == me, owner[1] == tile)
    send_or_keep(obs_home, send_obs, obs.at[1], ob_s.at[0], ob_r.at[0], owner)
    send_or_keep(obs_home, obs_index, index, ob_s.at[1], ob_r.at[1], owner)
    remote(send_w.at[0], recv_w.at[1], w_s.at[0], w_r.at[1], (me, left_tile)).start()
    remote(send_w.at[1], recv_w.at[0], w_s.at[1], w_r.at[0], (me, right_tile)).start()

    turn(1)
    turn(2)
    for step in (4, 3, 5, 2, 6, 1, 7, 0):
        g = lax.rem(z + step, GROUPS)
        there = ring_device(g, half)
        if step:
            remote(send_a.at[g, pl.ds(1, 2)], drift.at[me], ad_s.at[step], ad_r.at[me], there).start()
        else:
            send_or_keep(at_home, send_a.at[g, pl.ds(1, 2)], drift.at[me], ad_s.at[step], ad_r.at[me], there)

    settle(index, ob_r.at[1])
    cell = index[...].astype(F32)
    cell_row = jnp.floor((cell + 0.5) * (1.0 / SPAN))
    cell_col = cell - SPAN * cell_row
    row_at = iota((16, cell.shape[1]), 0).astype(F32)
    col_at = iota((3 * LANES, cell.shape[1]), 0).astype(F32)
    for p in range(PATCHES):
        rows = (row_at == cell_row[p : p + 1]).astype(F32).astype(BF16)
        cols = (col_at == cell_col[p : p + 1] + float(p * PC)).astype(F32).astype(BF16)
        hits = dot_lanes(rows, cols)
        for s in range(3):
            count[s, p] = hits[:RB, s * LANES : (s + 1) * LANES]

    settle(obs.at[1], ob_r.at[0])
    mate_slot = 2 * core
    side_slot = 2 - 2 * core
    remote(obs.at[1], obs.at[mate_slot], b_s.at[0, 8], b_r.at[mate_slot, 8], chip_mate).start()
    remote(obs.at[1], obs.at[side_slot], b_s.at[1, 8], b_r.at[side_slot, 8], side_mate).start()
    for j in range(GROUPS):
        settle(thick.at[1, j], at_r.at[j])
        remote(thick.at[1, j], thick.at[side_slot, j], b_s.at[1, j], b_r.at[side_slot, j], side_mate).start()
        remote(thick.at[1, j], thick.at[mate_slot, j], b_s.at[0, j], b_r.at[mate_slot, j], chip_mate).start()

    pad = iota((16, LANES), 0)

    def system_part(s, place):
        both = obs[s].astype(F32)
        values, variance = both[:RB], both[RB:]
        for p in range(PATCHES):
            weight[p] = count[s, p] / variance
        acc_values = values

        def rows_pair(pair, carry):
            two = thick[s, :, aligned(pair * 16, 16, 16), :].astype(F32)
            for h in range(2):
                r = pair * 2 + h
                x = two[:, h * 8 : h * 8 + 8, :].reshape(ENS, LANES)
                mean = jnp.sum(x, axis=0, keepdims=True) * (1.0 / ENS)
                anom = x - mean
                value = jnp.sum(jnp.where(iota((RB, LANES), 0) == r, acc_values, 0.0), axis=0, keepdims=True)
                extra = jnp.where(pad == 0, value - mean, 0.0)
                lanes = aligned((place * RB + r) * LANES, LANES, LANES)
                ext_hi, ext_lo = split(jnp.concatenate([anom, extra], axis=0))
                anom_hi[:, lanes] = ext_hi
                anom_lo[:, lanes] = ext_lo
                for p in range(PATCHES):
                    high, low = split(anom * weight[p, pl.ds(r, 1), :])
                    heavy_hi[p * ENS : (p + 1) * ENS, lanes] = high
                    heavy_lo[p * ENS : (p + 1) * ENS, lanes] = low
            return carry

        lax.fori_loop(0, RB // 2, rows_pair, 0)
        span = slice(place * RB * LANES, (place + 1) * RB * LANES)
        left = jnp.concatenate([anom_hi[:, span], anom_lo[:, span]], axis=0)
        main = dot_lanes(left, heavy_hi[:, span])
        rest = dot_lanes(anom_hi[:, span], heavy_lo[:, span])
        part = main[:80] + main[80:] + rest
        if place == 0:
            acc[...] = part
        else:
            acc[...] += part

    system_part(1, 0)
    for place, s in ((1, 2 - 2 * core), (2, 2 * core)):
        settle(obs.at[s], b_r.at[s, 8])
        for j in range(GROUPS):
            settle(thick.at[s, j], b_r.at[s, j])
        system_part(s, place)

    for j in range(GROUPS):
        settle(drift.at[j], ad_r.at[j])
    edge_lane = iota((ENS, LANES), 1)
    for v in range(FIELDS):
        for pair in range(RB // 2):
            rows = slice(pair * 16, pair * 16 + 16)
            two = (thick[1, :, rows, :] if v == 0 else drift[:, v - 1, rows, :]).astype(F32)
            for h in range(2):
                j = v * RB + pair * 2 + h
                x = two[:, h * 8 : h * 8 + 8, :].reshape(ENS, LANES)
                here = (edge_lane // HALO) == j
                low = pltpu.roll(x, (HALO * j) % LANES, 1)
                high = pltpu.roll(x, (HALO * j + HALO) % LANES, 1)
                if j == 0:
                    packed[0] = jnp.where(here, low, 0.0)
                    packed[1] = jnp.where(here, high, 0.0)
                else:
                    packed[0] = jnp.where(here, low, packed[0])
                    packed[1] = jnp.where(here, high, packed[1])
                for p in range(PATCHES):
                    masked[p * ENS : (p + 1) * ENS, j * LANES : (j + 1) * LANES] = jnp.where(
                        edge_lane // PC == p, x, 0.0
                    ).astype(BF16)

    weights = root_weights(acc[:ENS], acc[ENS:])
    left = jnp.concatenate(split(weights), axis=0)

    for side, p in ((0, 0), (1, PATCHES - 1)):
        edge = dot(left[:, p * ENS : (p + 1) * ENS], packed[side].astype(BF16))
        edge_send[side] = (edge[:ENS] + edge[ENS:]).astype(BF16)
    remote(edge_send.at[1 - core], edge_recv.at[core], n_s.at[0], n_r.at[core], chip_mate).start()
    remote(edge_send.at[core], edge_recv.at[1 - core], n_s.at[1], n_r.at[1 - core], side_mate).start()

    def member_device(step):
        to = lax.rem(me + step, GROUPS)
        return to, (to, ring * 2 + core)

    for v in range(FIELDS):
        for pair in range(RB // 2):
            at = (v * RB + pair * 2) * LANES
            got = dot(left, masked[:, at : at + 256])
            got = got[:ENS] + got[ENS:]
            for to in range(GROUPS):
                rows = slice(to * 8, to * 8 + 8)
                send_c[v, to, pair * 16 : pair * 16 + 16, :] = jnp.concatenate(
                    [got[rows, :LANES], got[rows, LANES:]], axis=0
                ).astype(BF16)
        for step in (4, 3, 5, 2, 6, 1, 7, 0):
            to, there = member_device(step)
            if step:
                remote(send_c.at[v, to], recv_c.at[v, z], c_s.at[v, step], c_r.at[v, z], there).start()
            else:
                send_or_keep(at_home, send_c.at[v, to], recv_c.at[v, z], c_s.at[v, step], c_r.at[v, z], there)
        if v == 1:
            for side in range(2):
                settle(edge_recv.at[side], n_r.at[side])
            for to in range(GROUPS):
                rows = slice(to * 8, to * 8 + 8)
                send_e[to] = jnp.concatenate(
                    [edge_recv[0].astype(F32)[rows], edge_recv[1].astype(F32)[rows]], axis=0
                ).astype(BF16)
            for step in (4, 3, 5, 2, 6, 1, 7, 0):
                to, there = member_device(step)
                if step:
                    remote(send_e.at[to], recv_e.at[z], e_s.at[step], e_r.at[z], there).start()
                else:
                    send_or_keep(at_home, send_e.at[to], recv_e.at[z], e_s.at[step], e_r.at[z], there)

    def strip(own, from_left, from_right, j):
        left_part = pltpu.roll(from_left, (LANES - HALO - HALO * j) % LANES, 1)
        right_part = pltpu.roll(from_right, (64 - HALO * j) % LANES, 1)
        outer = jnp.where(lane >= LANES - HALO, left_part, jnp.where(lane >= 64, right_part, pltpu.roll(own, 64, 1)))
        return jnp.where(lane < 2 * HALO, own, jnp.where(jnp.logical_and(lane >= 68, lane < 124), 0.0, outer))

    for side in range(2):
        settle(recv_w.at[side], w_r.at[side])
    for f, ref in ((0, mask_f), (1, tau_x), (2, tau_y)):
        whole = flat_field(f)
        if f == 0:
            whole = whole * (1.0 / 1.5)
        for g in range(GROUPS):
            own = whole[g * RB : (g + 1) * RB]
            gain = 1.0 / 1.5 if f == 0 else 1.0
            edges = strip(own, recv_w[0] * gain, recv_w[1] * gain, f * GROUPS + g)
            for r in range(RB):
                row = (g * RB + r) * 16
                ref[row : row + 8, :] = jnp.broadcast_to(own[r : r + 1], (8, LANES))
                ref[row + 8 : row + 16, :] = jnp.broadcast_to(edges[r : r + 1], (8, LANES))

    for ref in (field_x, field_y, normal_x, normal_y, shear):
        ref[0:16, :] = jnp.zeros((16, LANES), F32)
        ref[(ROWS + 1) * 16 :, :] = jnp.zeros((16, LANES), F32)

    for g in range(GROUPS):
        settle(recv_e.at[g], e_r.at[g])
        for v in range(FIELDS):
            settle(recv_c.at[v, g], c_r.at[v, g])

    def unpack(g, carry):
        edges = recv_e[g].astype(F32)
        for v in range(FIELDS):
            for pair in range(RB // 2):
                two = recv_c[v, g, pair * 16 : pair * 16 + 16, :].astype(F32)
                if v == 0:
                    final[0, aligned(g * 64 + pair * 16, 16, 16), :] = two
                for h in range(2):
                    r = pair * 2 + h
                    own = two[h * 8 : h * 8 + 8]
                    both = jnp.concatenate([own, strip(own, edges[:8], edges[8:], v * RB + r)], axis=0)
                    row = g * RB + r
                    if v == 0:
                        soft = jnp.maximum(both, 0.0) + jnp.log1p(jnp.exp(-jnp.abs(both)))
                        press[aligned(row * 16, 16, 16), :] = soft
                    else:
                        (field_x, field_y)[v - 1][aligned((row + 1) * 16, 16, 16), :] = both
        return carry

    lax.fori_loop(0, GROUPS, unpack, 0)

    block = 4

    def around(ref, at):
        start = at * block * 16
        return [ref[aligned(start + 16 * k, block * 16, 16), :] for k in range(3)]

    def slope_x(x):
        return 0.5 * (pltpu.roll(x, LANES - 1, 1) - pltpu.roll(x, 1, 1))

    for sweep in range(2):

        def stress(at, carry):
            x_up, x, x_down = around(field_x, at)
            y_up, y, y_down = around(field_y, at)
            p = press[aligned(at * block * 16, block * 16, 16), :]
            here = aligned((at * block + 1) * 16, block * 16, 16)
            dxx, dyx = slope_x(x), slope_x(y)
            dxy, dyy = 0.5 * (x_down - x_up), 0.5 * (y_down - y_up)
            half_p = 0.5 * p
            spread = half_p * (dxx + dyy) - 0.5 * half_p
            skew = (0.25 * half_p) * (dxx - dyy)
            turn_rate = (0.25 * p) * (dxy + dyx)
            new = (spread + skew, spread - skew, turn_rate)
            for ref, term in zip((normal_x, normal_y, shear), new):
                ref[here, :] = 0.5 * term if sweep == 0 else 0.5 * (ref[here, :] + term)
            return carry

        lax.fori_loop(0, ROWS // block, stress, 0)

        def move(at, carry):
            s_up, s, s_down = around(shear, at)
            n_up, _, n_down = around(normal_y, at)
            here = aligned((at * block + 1) * 16, block * 16, 16)
            flat = aligned(at * block * 16, block * 16, 16)
            free = mask_f[flat, :]
            force_x = slope_x(normal_x[here, :]) + 0.5 * (s_down - s_up) + tau_x[flat, :]
            force_y = slope_x(s) + 0.5 * (n_down - n_up) + tau_y[flat, :]
            new_x = free * (field_x[here, :] + 0.5 * force_x)
            new_y = free * (field_y[here, :] + 0.5 * force_y)
            if sweep == 0:
                field_x[here, :] = new_x
                field_y[here, :] = new_y
            else:
                for v, new in ((1, new_x), (2, new_y)):
                    new = new.reshape(block, 16, LANES)
                    main = new[:, :8].reshape(block * 8, LANES)
                    edge = new[:, 8:].reshape(block * 8, LANES)
                    at_lane = iota((block * 8, LANES), 1)
                    main = jnp.where(at_lane < HALO, edge, main)
                    main = jnp.where(at_lane >= LANES - HALO, pltpu.roll(edge, 64, 1), main)
                    final[v, aligned(at * block * 8, block * 8, 8), :] = main
            return carry

        lax.fori_loop(0, ROWS // block, move, 0)

    for v in range(FIELDS):
        for j in range(GROUPS):
            for start in range(0, ROWS, 16):
                parts = [final[v, pl.ds((start + h * 8) * 8 + j, 8, stride=8), :] for h in range(2)]
                out[j, v, start : start + 16, :] = jnp.concatenate(parts, axis=0).astype(BF16)

    for step in range(GROUPS):
        g = lax.rem(z + step, GROUPS)
        same = at_home if step == 0 else False
        to, _ = member_device(step)
        pairs = [(send_a.at[g, 0], at_s.at[step]), (send_a.at[g, pl.ds(1, 2)], ad_s.at[step]), (send_e.at[to], e_s.at[step])]
        pairs += [(send_c.at[v, to], c_s.at[v, step]) for v in range(FIELDS)]
        for src, sem in pairs:
            if step == 0:
                wait_sent(at_home, src, sem)
            else:
                settle(src, sem)
    wait_sent(obs_home, send_obs, ob_s.at[0])
    wait_sent(obs_home, obs_index, ob_s.at[1])
    for side in range(2):
        settle(send_w.at[side], w_s.at[side])
        settle(obs.at[1], b_s.at[side, 8])
        settle(edge_send.at[side], n_s.at[side])
        for j in range(GROUPS):
            settle(thick.at[1, j], b_s.at[side, j])


def body(tiles, background, obs_value, obs_var, obs_index, ice_mask, wind_stress):
    vmem = pl.BlockSpec(memory_space=pltpu.VMEM)
    dma = pltpu.SemaphoreType.DMA
    rows = (ROWS + 2) * 16
    return pl.pallas_call(
        functools.partial(kernel, tiles),
        out_shape=jax.ShapeDtypeStruct(background.shape, BF16),
        in_specs=[vmem] * 6,
        out_specs=vmem,
        scratch_shapes=[
            pltpu.VMEM((GROUPS * ROWS, LANES), F32),
            pltpu.VMEM((GROUPS, FIELDS, 64, LANES), BF16),
            pltpu.VMEM((16, LANES), BF16),
            pltpu.VMEM((3, GROUPS, 64, LANES), BF16),
            pltpu.VMEM((GROUPS, 2, 64, LANES), BF16),
            pltpu.VMEM((3, 16, LANES), BF16),
            pltpu.VMEM((PATCHES, obs_index.shape[2]), jnp.int32),
            pltpu.VMEM((3, PATCHES, RB, LANES), F32),
            pltpu.VMEM((PATCHES, RB, LANES), F32),
            pltpu.VMEM((80, CELLS), BF16),
            pltpu.VMEM((80, CELLS), BF16),
            pltpu.VMEM((WIDE, CELLS), BF16),
            pltpu.VMEM((WIDE, CELLS), BF16),
            pltpu.VMEM((80, WIDE), F32),
            pltpu.VMEM((WIDE, FIELDS * RB * LANES), BF16),
            pltpu.VMEM((2, ENS, LANES), F32),
            pltpu.VMEM((2, ENS, LANES), BF16),
            pltpu.VMEM((2, ENS, LANES), BF16),
            pltpu.VMEM((FIELDS, GROUPS, 64, LANES), BF16),
            pltpu.VMEM((FIELDS, GROUPS, 64, LANES), BF16),
            pltpu.VMEM((GROUPS, 16, LANES), BF16),
            pltpu.VMEM((GROUPS, 16, LANES), BF16),
            pltpu.VMEM((2, RB, LANES), F32),
            pltpu.VMEM((2, RB, LANES), F32),
            pltpu.VMEM((ROWS * 16, LANES), F32),
            pltpu.VMEM((ROWS * 16, LANES), F32),
            pltpu.VMEM((ROWS * 16, LANES), F32),
            pltpu.VMEM((ROWS * 16, LANES), F32),
            pltpu.VMEM((rows, LANES), F32),
            pltpu.VMEM((rows, LANES), F32),
            pltpu.VMEM((rows, LANES), F32),
            pltpu.VMEM((rows, LANES), F32),
            pltpu.VMEM((rows, LANES), F32),
            pltpu.VMEM((FIELDS, ROWS * 8, LANES), F32),
            dma((GROUPS,)), dma((GROUPS,)),
            dma((GROUPS,)), dma((GROUPS,)),
            dma((2,)), dma((2,)),
            dma((2, 9)), dma((3, 9)),
            dma((2,)), dma((2,)),
            dma((FIELDS, GROUPS)), dma((FIELDS, GROUPS)),
            dma((GROUPS,)), dma((GROUPS,)),
            dma((2,)), dma((2,)),
        ],
        compiler_params=pltpu.CompilerParams(
            collective_id=0, has_side_effects=True, vmem_limit_bytes=50 * 1024 * 1024
        ),
        name="analysis_and_drift",
    )(background, obs_value, obs_var, obs_index[0], ice_mask, wind_stress)


def solution(mesh):
    placed = (
        P("mem", None, None, "tile"),
        P("mem", "tile"),
        P("mem", "tile"),
        P("mem", "tile", None),
        P(None, "tile"),
        P(None, None, "tile"),
    )
    return jax.shard_map(
        functools.partial(body, mesh.shape["tile"]),
        mesh=mesh,
        in_specs=placed,
        out_specs=P("mem", None, None, "tile"),
        check_vma=False,
    )
```

time: 250 us -> 61.7 us (0.25)
  the two profiles are of different devices: /device:TPU:4 before, /device:TPU:1 now
where the time goes in v1:
time: 61.7 us; the launch traced here: 61.3 us
  Pallas kernels  56 us (91%)
  local copies, waits for them, and re-layouts  5.32 us (9%)
    pallas_call x1, Pallas kernels, body(): pl.pallas_call(functools.partial(kernel, tiles), out_shape=jax.ShapeDtype...  56 us
    unnamed x13, local copies, waits for them, and re-layouts  5.32 us

profile of v1, /device:TPU:1, one launch (start us, length us, event | category | flops | bytes accessed | tf_op | source)
XLA Modules:
  0.0 61.3 jit_solution(15559769218603892412)
XLA Ops:
  0.0 0.0 copy-start
  0.0 1.0 %copy-done = bf16[8,3,64,128]{3,2,1,0:T(8,128)(2,1)S(1)} copy-done((bf16[8,3,64,128]{3,2,1,0:T(8,128)(2,1)S(1)}, bf16[8,3,64,128]{3,2,1,0:T(8,128)(2,1)}, u32[]{:S(2)}) %copy-start) | copy-done | bytes 393240
  1.0 0.0 copy-start.1
  1.0 0.8 %copy-done.1 = s32[64,128]{1,0:T(8,128)S(1)} copy-done((s32[64,128]{1,0:T(8,128)S(1)}, s32[64,128]{1,0:T(8,128)}, u32[]{:S(2)}) %copy-start.1) | copy-done | bytes 32792
  1.8 0.0 copy-start.2
  1.8 0.8 %copy-done.2 = bf16[2,64,128]{2,1,0:T(8,128)(2,1)S(1)} copy-done((bf16[2,64,128]{2,1,0:T(8,128)(2,1)S(1)}, bf16[2,64,128]{2,1,0:T(8,128)(2,1)}, u32[]{:S(2)}) %copy-start.2) | copy-done | bytes 32792
  2.5 0.0 copy-start.3
  2.5 0.7 %copy-done.3 = s32[1,8,256]{2,1,0:T(8,128)S(1)} copy-done((s32[1,8,256]{2,1,0:T(8,128)S(1)}, s32[1,8,256]{2,1,0:T(8,128)}, u32[]{:S(2)}) %copy-start.3) | copy-done | bytes 8216
  3.2 0.0 copy-start.4
  3.2 0.7 %copy-done.4 = bf16[8,128]{1,0:T(8,128)(2,1)S(1)} copy-done((bf16[8,128]{1,0:T(8,128)(2,1)S(1)}, bf16[8,128]{1,0:T(8,128)(2,1)}, u32[]{:S(2)}) %copy-start.4) | copy-done | bytes 2072
  3.9 0.0 copy-start.5
  3.9 0.7 %copy-done.5 = bf16[8,128]{1,0:T(8,128)(2,1)S(1)} copy-done((bf16[8,128]{1,0:T(8,128)(2,1)S(1)}, bf16[8,128]{1,0:T(8,128)(2,1)}, u32[]{:S(2)}) %copy-start.5) | copy-done | bytes 2072
  4.6 56.0 %analysis_and_drift.1 = bf16[8,3,64,128]{3,2,1,0:T(8,128)(2,1)S(1)} custom-call(bf16[8,3,64,128]{3,2,1,0:T(8,128)(2,1)S(1)} %copy-done, bf16[8,128]{1,0:T(8,128)(2,1)S(1)} %copy-done.4, bf16[8,128]{1,0:T(8,128)(2,1)S(1)} %copy-done.5, s32[8,256]{1,0:T(8,128)S(1)} %bitcast.1, s32[64,128]{1,0:T(8,128)S(1)} %copy-done.1, bf16[2,64,128]{2,1,0:T(8,128)(2,1)S(1)} %copy-done.2), custom_call_target="tpu_custom_call" | custom-call | tf_op jit(solution)/shard_map/analysis_and_drift/pallas_call | solution.py:485
  60.6 0.7 %copy.8 = bf16[8,3,64,128]{3,2,1,0:T(8,128)(2,1)} copy(bf16[8,3,64,128]{3,2,1,0:T(8,128)(2,1)S(1)} %analysis_and_drift.1) | data formatting | bytes 786432
Async XLA Ops:
  0.0 1.0 %copy-start = (bf16[8,3,64,128]{3,2,1,0:T(8,128)(2,1)S(1)}, bf16[8,3,64,128]{3,2,1,0:T(8,128)(2,1)}, u32[]{:S(2)}) copy-start(bf16[8,3,64,128]{3,2,1,0:T(8,128)(2,1)} %bg.1) | copy-start | bytes 1179652
  1.0 0.8 %copy-start.1 = (s32[64,128]{1,0:T(8,128)S(1)}, s32[64,128]{1,0:T(8,128)}, u32[]{:S(2)}) copy-start(s32[64,128]{1,0:T(8,128)} %ice_mask.1) | copy-start | bytes 98308
  1.8 0.8 %copy-start.2 = (bf16[2,64,128]{2,1,0:T(8,128)(2,1)S(1)}, bf16[2,64,128]{2,1,0:T(8,128)(2,1)}, u32[]{:S(2)}) copy-start(bf16[2,64,128]{2,1,0:T(8,128)(2,1)} %wind.1) | copy-start | bytes 98308
  2.5 0.7 %copy-start.3 = (s32[1,8,256]{2,1,0:T(8,128)S(1)}, s32[1,8,256]{2,1,0:T(8,128)}, u32[]{:S(2)}) copy-start(s32[1,8,256]{2,1,0:T(8,128)} %param.9) | copy-start | bytes 24580
  3.2 0.7 %copy-start.4 = (bf16[8,128]{1,0:T(8,128)(2,1)S(1)}, bf16[8,128]{1,0:T(8,128)(2,1)}, u32[]{:S(2)}) copy-start(bf16[8,128]{1,0:T(8,128)(2,1)} %obs_value.1) | copy-start | bytes 6148
  3.9 0.7 %copy-start.5 = (bf16[8,128]{1,0:T(8,128)(2,1)S(1)}, bf16[8,128]{1,0:T(8,128)(2,1)}, u32[]{:S(2)}) copy-start(bf16[8,128]{1,0:T(8,128)(2,1)} %obs_var.1) | copy-start | bytes 6148

commit v2 on v1

v2 whole, which is shorter than its diff:
```python
import functools

import jax
import jax.numpy as jnp
from jax import lax
from jax.experimental import pallas as pl
from jax.experimental.pallas import tpu as pltpu
from jax.sharding import PartitionSpec as P

F32 = jnp.float32
BF16 = jnp.bfloat16
MESH = pl.DeviceIdType.MESH

ENS = 64
GROUPS = 8
RB = 8
ROWS = 64
PC = 16
W = 128
SPAN = PC + 2 * W
LANES = 128
PATCHES = 8
FIELDS = 3
NS_ITERS = 6
WIDE = PATCHES * ENS
CELLS = 3 * RB * LANES
HALO = 4
EDGE_ROWS = 4
STRIP_ROWS = 16 + 2 * EDGE_ROWS


def iota(shape, axis):
    return lax.broadcasted_iota(jnp.int32, shape, axis)


def aligned(start, size, by):
    return pl.ds(pl.multiple_of(start, by), size)


def split(x):
    high = x.astype(BF16)
    return high, (x - high.astype(F32)).astype(BF16)


def dot(a, b):
    return jnp.dot(a, b, preferred_element_type=F32)


def dot_lanes(a, b):
    return lax.dot_general(a, b, (((1,), (1,)), ((), ())), preferred_element_type=F32)


def block_diagonal(x):
    segment = iota(x.shape, 1) // ENS
    zero = jnp.zeros_like(x)
    return jnp.concatenate([jnp.where(segment == q, x, zero) for q in range(4)], axis=0)


def patch_products(left, right):
    rows = left.shape[0]
    left_high, left_low = split(left)
    right_high, right_low = split(right)
    out = []
    for half in range(2):
        lanes = slice(half * 256, (half + 1) * 256)
        both = jnp.concatenate([left_high[:, lanes], left_low[:, lanes]], axis=0)
        main = dot(both, block_diagonal(right_high[:, lanes]))
        rest = dot(left_high[:, lanes], block_diagonal(right_low[:, lanes]))
        out.append(main[:rows] + main[rows:] + rest)
    return jnp.concatenate(out, axis=1)


def root_weights(system, projected):
    row = iota((ENS, WIDE), 0)
    eye = ((iota((ENS, WIDE), 1) % ENS) == row).astype(F32)
    full = system + (ENS - 1.0) * eye
    squares = jnp.sum(full * full, axis=0, keepdims=True)
    own = ((iota((PATCHES, WIDE), 1) // ENS) == iota((PATCHES, WIDE), 0)).astype(F32)
    norm = jnp.sum(own * squares, axis=1, keepdims=True)
    scale = jnp.sqrt(jnp.sum(own * norm, axis=0, keepdims=True))
    centring = eye - 1.0 / ENS
    iterate = (system + (ENS - 1.0) * centring) / scale
    factor = 1.5 * eye - 0.5 * iterate
    inverse_root = 1.5 * centring - 0.5 * iterate
    moved = patch_products(jnp.concatenate([iterate, projected], axis=0), factor)
    iterate, projected = moved[:ENS], moved[ENS:]
    for sweep in range(1, NS_ITERS):
        factor = 1.5 * eye - 0.5 * patch_products(inverse_root, iterate)
        if sweep < NS_ITERS - 1:
            moved = patch_products(jnp.concatenate([iterate, inverse_root, projected], axis=0), factor)
            iterate, inverse_root, projected = moved[:ENS], moved[ENS : 2 * ENS], moved[2 * ENS :]
        else:
            moved = patch_products(jnp.concatenate([inverse_root, projected], axis=0), factor)
            inverse_root, projected = moved[:ENS], moved[ENS:]
    mean_weight = patch_products(projected, inverse_root)[:1] / scale
    return jnp.sqrt(ENS - 1.0) * (inverse_root / jnp.sqrt(scale)) + (mean_weight + 1.0 / ENS)


def kernel(
    tiles,
    prior, obs_value_hbm, obs_var_hbm, obs_index, mask_hbm, wind_hbm,
    out_hbm,
    obs_value, obs_var, ice_mask, wind,
    tall, send_obs, thick, drift, obs, index,
    count, weight, anom_hi, anom_lo, heavy_hi, heavy_lo, acc,
    masked, packed, edge_send, edge_recv,
    send_c, recv_c, send_e, recv_e,
    send_w, recv_w, padded, flat_halo, strip_halo,
    free, tau_x, tau_y, press, field_x, field_y, normal_x, normal_y, shear,
    strip_free, strip_tau_x, strip_tau_y, strip_press, strip_x, strip_y, strip_normal_x, strip_normal_y, strip_shear,
    final, result,
    in_s, out_s, at_s, at_r, ad_s, ad_r, ob_s, ob_r, b_s, b_r, n_s, n_r, c_s, c_r, e_s, e_r, w_s, w_r,
):
    me, tile = lax.axis_index("mem"), lax.axis_index("tile")
    core, z_lo = me % 2, me // 2
    half, ring = tile % 2, tile // 2
    z = half * 4 + z_lo

    def ring_device(at_z, at_core):
        return ((at_z % 4) * 2 + at_core, ring * 2 + at_z // 4)

    chip_mate = (me + 1 - 2 * core, tile)
    side_mate = (me + 1 - 2 * core, lax.rem(tile + tiles - 2 + 4 * core, tiles))
    left_tile = lax.rem(tile + tiles - 1, tiles)
    right_tile = lax.rem(tile + 1, tiles)
    outer_tile = jnp.where(half == 0, left_tile, right_tile)

    loads = [
        pltpu.make_async_copy(src, dst, in_s.at[i])
        for i, (src, dst) in enumerate(
            (
                (obs_value_hbm, obs_value),
                (obs_var_hbm, obs_var),
                (mask_hbm, ice_mask),
                (wind_hbm, wind),
            )
        )
    ]
    for load in loads:
        load.start()

    barrier = pltpu.get_barrier_semaphore()

    def greet(step, carry):
        at = lax.rem(z * 2 + core + lax.rem(step + 7, 15) + 1, 16)
        pl.semaphore_signal(barrier, inc=1, device_id=ring_device(at // 2, at % 2), device_id_type=MESH)
        return carry

    lax.fori_loop(1, 16, greet, 0)
    pl.semaphore_signal(barrier, inc=1, device_id=side_mate, device_id_type=MESH)
    pl.semaphore_signal(barrier, inc=1, device_id=(me, outer_tile), device_id_type=MESH)

    lane = iota((RB, LANES), 1)

    pl.semaphore_wait(barrier, 17)

    def remote(src, dst, s_sem, r_sem, device):
        return pltpu.make_async_remote_copy(
            src_ref=src, dst_ref=dst, send_sem=s_sem, recv_sem=r_sem, device_id=device, device_id_type=MESH
        )

    def settle(ref, sem):
        pltpu.make_async_copy(ref, ref, sem).wait()

    def send_or_keep(same, src, dst, s_sem, r_sem, device):
        @pl.when(same)
        def _():
            pltpu.make_async_copy(src, dst, r_sem).start()

        @pl.when(jnp.logical_not(same))
        def _():
            remote(src, dst, s_sem, r_sem, device).start()

    def wait_sent(same, src, s_sem):
        @pl.when(jnp.logical_not(same))
        def _():
            settle(src, s_sem)

    at_home = core == half
    far_first = (4, 3, 5, 2, 6, 1, 7, 0)
    for step in far_first:
        g = lax.rem(z + step, GROUPS)
        there = ring_device(g, half)
        if step:
            remote(prior.at[:, 0, g], thick.at[1, me], at_s.at[step], at_r.at[me], there).start()
        else:
            send_or_keep(at_home, prior.at[:, 0, g], thick.at[1, me], at_s.at[step], at_r.at[me], there)
    owner = ring_device(me, half)
    obs_home = jnp.logical_and(owner[0] == me, owner[1] == tile)
    send_or_keep(obs_home, obs_index, index, ob_s.at[1], ob_r.at[1], owner)
    for load in loads:
        load.wait()
    send_obs[...] = jnp.concatenate([obs_value[...].astype(F32), obs_var[...].astype(F32)], axis=0).astype(BF16)
    send_or_keep(obs_home, send_obs, obs.at[1], ob_s.at[0], ob_r.at[0], owner)
    def flat_field(f):
        return ice_mask[...].astype(F32) if f == 0 else wind[f - 1].astype(F32)

    low = jnp.zeros((RB, LANES), F32)
    high = jnp.zeros((RB, LANES), F32)
    for f in range(FIELDS):
        whole = flat_field(f)
        for g in range(GROUPS):
            j = f * GROUPS + g
            rows = whole[g * RB : (g + 1) * RB]
            here = (lane // HALO) == j
            low = jnp.where(here, pltpu.roll(rows, (HALO * j) % LANES, 1), low)
            high = jnp.where(here, pltpu.roll(rows, (HALO * j + HALO) % LANES, 1), high)
    send_w[0] = low
    send_w[1] = high

    remote(send_w.at[0], recv_w.at[1], w_s.at[0], w_r.at[1], (me, left_tile)).start()
    remote(send_w.at[1], recv_w.at[0], w_s.at[1], w_r.at[0], (me, right_tile)).start()

    settle(index, ob_r.at[1])
    cell = index[...].astype(F32)
    cell_row = jnp.floor((cell + 0.5) * (1.0 / SPAN))
    cell_col = cell - SPAN * cell_row
    row_at = iota((16, cell.shape[1]), 0).astype(F32)
    col_at = iota((3 * LANES, cell.shape[1]), 0).astype(F32)
    for p in range(PATCHES):
        rows = (row_at == cell_row[p : p + 1]).astype(F32).astype(BF16)
        cols = (col_at == cell_col[p : p + 1] + float(p * PC)).astype(F32).astype(BF16)
        hits = dot_lanes(rows, cols)
        for s in range(3):
            count[s, p] = hits[:RB, s * LANES : (s + 1) * LANES]

    settle(obs.at[1], ob_r.at[0])
    mate_slot = 2 * core
    side_slot = 2 - 2 * core
    remote(obs.at[1], obs.at[mate_slot], b_s.at[0, 8], b_r.at[mate_slot, 8], chip_mate).start()
    remote(obs.at[1], obs.at[side_slot], b_s.at[1, 8], b_r.at[side_slot, 8], side_mate).start()
    for j in range(GROUPS):
        settle(thick.at[1, j], at_r.at[j])
        remote(thick.at[1, j], thick.at[side_slot, j], b_s.at[1, j], b_r.at[side_slot, j], side_mate).start()
        remote(thick.at[1, j], thick.at[mate_slot, j], b_s.at[0, j], b_r.at[mate_slot, j], chip_mate).start()

    for step in far_first:
        g = lax.rem(z + step, GROUPS)
        there = ring_device(g, half)
        if step:
            remote(prior.at[:, pl.ds(1, 2), g], drift.at[me], ad_s.at[step], ad_r.at[me], there).start()
        else:
            send_or_keep(at_home, prior.at[:, pl.ds(1, 2), g], drift.at[me], ad_s.at[step], ad_r.at[me], there)

    pad = iota((16, LANES), 0)

    def system_part(s, place):
        both = obs[s].astype(F32)
        values, variance = both[:RB], both[RB:]
        for p in range(PATCHES):
            weight[p] = count[s, p] / variance
        tall[place] = thick[s].astype(F32).reshape(ENS * RB, LANES)

        def rows_pair(pair, carry):
            for h in range(2):
                r = pair * 2 + h
                x = tall[place, pl.ds(r, ENS, stride=RB), :]
                mean = jnp.sum(x, axis=0, keepdims=True) * (1.0 / ENS)
                anom = x - mean
                value = jnp.sum(jnp.where(iota((RB, LANES), 0) == r, values, 0.0), axis=0, keepdims=True)
                extra = jnp.where(pad == 0, value - mean, 0.0)
                lanes = aligned((place * RB + r) * LANES, LANES, LANES)
                ext_hi, ext_lo = split(jnp.concatenate([anom, extra], axis=0))
                anom_hi[:, lanes] = ext_hi
                anom_lo[:, lanes] = ext_lo
                for p in range(PATCHES):
                    high, low = split(anom * weight[p, pl.ds(r, 1), :])
                    heavy_hi[p * ENS : (p + 1) * ENS, lanes] = high
                    heavy_lo[p * ENS : (p + 1) * ENS, lanes] = low
            return carry

        lax.fori_loop(0, RB // 2, rows_pair, 0)
        span = slice(place * RB * LANES, (place + 1) * RB * LANES)
        left = jnp.concatenate([anom_hi[:, span], anom_lo[:, span]], axis=0)
        main = dot_lanes(left, heavy_hi[:, span])
        rest = dot_lanes(anom_hi[:, span], heavy_lo[:, span])
        part = main[:80] + main[80:] + rest
        if place == 0:
            acc[...] = part
        else:
            acc[...] += part

    system_part(1, 0)
    for place, s in ((1, 2 - 2 * core), (2, 2 * core)):
        settle(obs.at[s], b_r.at[s, 8])
        for j in range(GROUPS):
            settle(thick.at[s, j], b_r.at[s, j])
        system_part(s, place)

    edge_lane = iota((ENS, LANES), 1)

    def spread(v):
        for r in range(RB):
            j = v * RB + r
            x = tall[v, pl.ds(r, ENS, stride=RB), :]
            here = (edge_lane // HALO) == j
            low = pltpu.roll(x, (HALO * j) % LANES, 1)
            high = pltpu.roll(x, (HALO * j + HALO) % LANES, 1)
            if j == 0:
                packed[0] = jnp.where(here, low, 0.0)
                packed[1] = jnp.where(here, high, 0.0)
            else:
                packed[0] = jnp.where(here, low, packed[0])
                packed[1] = jnp.where(here, high, packed[1])
            for p in range(PATCHES):
                masked[p * ENS : (p + 1) * ENS, j * LANES : (j + 1) * LANES] = jnp.where(
                    edge_lane // PC == p, x, 0.0
                ).astype(BF16)

    spread(0)
    weights = root_weights(acc[:ENS], acc[ENS:])
    left = jnp.concatenate(split(weights), axis=0)

    def member_device(step):
        to = lax.rem(me + step, GROUPS)
        return to, (to, ring * 2 + core)

    for v in range(FIELDS):
        if v == 1:
            for j in range(GROUPS):
                settle(drift.at[j], ad_r.at[j])
            for f in (1, 2):
                tall[f] = drift[:, :, f - 1].astype(F32).reshape(ENS * RB, LANES)
                spread(f)
            for side, p in ((0, 0), (1, PATCHES - 1)):
                edge = dot(left[:, p * ENS : (p + 1) * ENS], packed[side].astype(BF16))
                edge_send[side] = (edge[:ENS] + edge[ENS:]).astype(BF16)
            remote(edge_send.at[1 - core], edge_recv.at[core], n_s.at[0], n_r.at[core], chip_mate).start()
            remote(edge_send.at[core], edge_recv.at[1 - core], n_s.at[1], n_r.at[1 - core], side_mate).start()
        if v == 2:
            for side in range(2):
                settle(edge_recv.at[side], n_r.at[side])
            for to in range(GROUPS):
                rows = slice(to * 8, to * 8 + 8)
                send_e[to] = jnp.concatenate(
                    [edge_recv[0].astype(F32)[rows], edge_recv[1].astype(F32)[rows]], axis=0
                ).astype(BF16)
            for step in far_first:
                to, there = member_device(step)
                if step:
                    remote(send_e.at[to], recv_e.at[z], e_s.at[step], e_r.at[z], there).start()
                else:
                    send_or_keep(at_home, send_e.at[to], recv_e.at[z], e_s.at[step], e_r.at[z], there)
        for pair in range(RB // 2):
            at = (v * RB + pair * 2) * LANES
            got = dot(left, masked[:, at : at + 256])
            got = got[:ENS] + got[ENS:]
            for to in range(GROUPS):
                rows = slice(to * 8, to * 8 + 8)
                send_c[v, to, pair * 16 : pair * 16 + 16, :] = jnp.concatenate(
                    [got[rows, :LANES], got[rows, LANES:]], axis=0
                ).astype(BF16)
        for step in far_first:
            to, there = member_device(step)
            if step:
                remote(send_c.at[v, to], recv_c.at[v, aligned(EDGE_ROWS * 8 + z * 64, 64, 16)], c_s.at[v, step], c_r.at[v, z], there).start()
            else:
                send_or_keep(at_home, send_c.at[v, to], recv_c.at[v, aligned(EDGE_ROWS * 8 + z * 64, 64, 16)], c_s.at[v, step], c_r.at[v, z], there)
    at_lane = iota((8, LANES), 1)
    lane_group, lane_in = at_lane // 32, at_lane % 32
    is_right = jnp.logical_and(lane_in >= 8, lane_in < 12)
    is_left = jnp.logical_and(lane_in >= 12, lane_in < 16)

    def strip_edges(from_left, from_right, j, q):
        left_part = pltpu.roll(from_left, (32 * q + 12 - HALO * j) % LANES, 1)
        right_part = pltpu.roll(from_right, (32 * q + 8 - HALO * j) % LANES, 1)
        here = lane_group == q
        part = jnp.where(jnp.logical_and(here, is_left), left_part, 0.0)
        return jnp.where(jnp.logical_and(here, is_right), right_part, part)

    pick_row, pick_lane = iota((4 * LANES, LANES), 0), iota((4 * LANES, LANES), 1)
    pick_col, pick_in = pick_row % LANES, pick_lane % 32
    wanted = jnp.where(pick_in < 8, 120 + pick_in, jnp.where(jnp.logical_and(pick_in >= 16, pick_in < 24), pick_in - 16, -1))
    picks = jnp.logical_and(pick_row // LANES == pick_lane // 32, pick_col == wanted).astype(F32).astype(BF16)

    for side in range(2):
        settle(recv_w.at[side], w_r.at[side])
    for f, (ref, strip_ref) in enumerate(((free, strip_free), (tau_x, strip_tau_x), (tau_y, strip_tau_y))):
        gain = 1.0 / 1.5 if f == 0 else 0.5
        whole = flat_field(f)
        for row in range(ROWS):
            ref[row * 8 : row * 8 + 8, :] = jnp.broadcast_to(whole[row : row + 1] * gain, (8, LANES))
        padded[0:8, :] = jnp.zeros((8, LANES), F32)
        padded[8 + ROWS :, :] = jnp.zeros((8, LANES), F32)
        padded[8 : 8 + ROWS, :] = whole
        parts = [padded[4 + 16 * q : 4 + 16 * q + STRIP_ROWS, :].astype(BF16) for q in range(4)]
        own = dot(jnp.concatenate(parts, axis=1), picks)
        flat_halo[...] = jnp.zeros(flat_halo.shape, F32)
        for q in range(4):
            for g in range(max(0, 2 * q - 1), min(GROUPS, 2 * q + 3)):
                start = 8 + 8 * g - 16 * q + EDGE_ROWS
                flat_halo[start : start + 8, :] += strip_edges(recv_w[0], recv_w[1], f * GROUPS + g, q)
        whole = (own + flat_halo[8 : 8 + STRIP_ROWS, :]) * gain
        for row in range(STRIP_ROWS):
            strip_ref[row * 8 : row * 8 + 8, :] = jnp.broadcast_to(whole[row : row + 1], (8, LANES))

    none = jnp.zeros((8, LANES), F32)
    for ref in (field_x, field_y, normal_x, normal_y, shear):
        ref[0:8, :] = none
        ref[(ROWS + 1) * 8 :, :] = none
    for ref in (strip_x, strip_y, strip_normal_x, strip_normal_y, strip_shear):
        ref[0:8, :] = none
        ref[(STRIP_ROWS + 1) * 8 :, :] = none
    for v in range(FIELDS):
        recv_c[v, 0 : EDGE_ROWS * 8, :] = jnp.zeros((EDGE_ROWS * 8, LANES), BF16)
        recv_c[v, (EDGE_ROWS + ROWS) * 8 :, :] = jnp.zeros((EDGE_ROWS * 8, LANES), BF16)

    for g in range(GROUPS):
        settle(recv_e.at[g], e_r.at[g])
    for row in range(STRIP_ROWS):
        for v in range(FIELDS):
            total = none
            for q in range(4):
                at = 16 * q - EDGE_ROWS + row
                if 0 <= at < ROWS:
                    edges = recv_e[at // RB].astype(F32)
                    total = total + strip_edges(edges[:8], edges[8:], v * RB + at % RB, q)
            strip_halo[v, row * 8 : row * 8 + 8, :] = total

    def pressure(x):
        return 0.125 * (jnp.maximum(x, 0.0) + jnp.log1p(jnp.exp(-jnp.abs(x))))

    strip_rows = STRIP_ROWS * 8
    for v in range(FIELDS):
        for g in range(GROUPS):
            settle(recv_c.at[v, pl.ds(EDGE_ROWS * 8 + g * 64, 64)], c_r.at[v, g])
        parts = [recv_c[v, 128 * q : 128 * q + strip_rows, :] for q in range(4)]
        strip = dot(jnp.concatenate(parts, axis=1), picks) + strip_halo[v]
        main = recv_c[v, EDGE_ROWS * 8 : (EDGE_ROWS + ROWS) * 8, :].astype(F32)
        if v == 0:
            row = iota((strip_rows, LANES), 0) // 8
            group = iota((strip_rows, LANES), 1) // 32
            outside = jnp.logical_or(
                jnp.logical_and(group == 0, row < EDGE_ROWS), jnp.logical_and(group == 3, row >= STRIP_ROWS - EDGE_ROWS)
            )
            strip_press[...] = jnp.where(outside, 0.0, pressure(strip))
            press[...] = pressure(main)
            final[0] = main
        else:
            (strip_x, strip_y)[v - 1][8 : 8 + strip_rows, :] = strip
            (field_x, field_y)[v - 1][8 : 8 + ROWS * 8, :] = main

    def difference(x):
        return pltpu.roll(x, LANES - 1, 1) - pltpu.roll(x, 1, 1)

    main_refs = (field_x, field_y, normal_x, normal_y, shear, press, free, tau_x, tau_y)
    strip_refs = (
        strip_x, strip_y, strip_normal_x, strip_normal_y, strip_shear, strip_press, strip_free, strip_tau_x, strip_tau_y,
    )
    height = 64
    blocks = [(main_refs, i) for i in range(ROWS * 8 // height)]
    for i in range(strip_rows // height):
        blocks.insert(3 * i + 2, (strip_refs, i))

    for sweep in range(2):
        for refs, i in blocks:
            f_x, f_y, n_x, n_y, s_xy, p_ref = refs[:6]
            up, here, down = (slice(i * height + 8 * k, (i + 1) * height + 8 * k) for k in range(3))
            across_x, across_y = difference(f_x[here, :]), difference(f_y[here, :])
            along_x = f_x[down, :] - f_x[up, :]
            along_y = f_y[down, :] - f_y[up, :]
            p = p_ref[up, :]
            spread = across_x + along_y - 1.0
            skew = 0.25 * (across_x - along_y)
            new = (p * (spread + skew), p * (spread - skew), (0.5 * p) * (along_x + across_y))
            for ref, term in zip((n_x, n_y, s_xy), new):
                ref[here, :] = term if sweep == 0 else 0.5 * ref[here, :] + term
        for refs, i in blocks:
            f_x, f_y, n_x, n_y, s_xy, _, open_ref, t_x, t_y = refs
            up, here, down = (slice(i * height + 8 * k, (i + 1) * height + 8 * k) for k in range(3))
            force_x = difference(n_x[here, :]) + (s_xy[down, :] - s_xy[up, :])
            force_y = difference(s_xy[here, :]) + (n_y[down, :] - n_y[up, :])
            f_x[here, :] = open_ref[up, :] * (f_x[here, :] + t_x[up, :] + 0.25 * force_x)
            f_y[here, :] = open_ref[up, :] * (f_y[here, :] + t_y[up, :] + 0.25 * force_y)

    writes = [pltpu.make_async_copy(result.at[:, v], out_hbm.at[:, v], out_s.at[v]) for v in range(FIELDS)]
    for v in range(FIELDS):
        if v:
            ref, strip_ref = ((field_x, strip_x), (field_y, strip_y))[v - 1]
            for row in range(0, ROWS, 4):
                q, at = row // 16, row % 16 + EDGE_ROWS + 1
                main = ref[(row + 1) * 8 : (row + 5) * 8, :]
                edge = strip_ref[at * 8 : at * 8 + 32, :]
                col = iota((32, LANES), 1)
                main = jnp.where(col < HALO, pltpu.roll(edge, (LANES - 32 * q - 16) % LANES, 1), main)
                main = jnp.where(col >= LANES - HALO, pltpu.roll(edge, (120 - 32 * q) % LANES, 1), main)
                final[v, row * 8 : row * 8 + 32, :] = main
        for j in range(GROUPS):
            for start in range(0, ROWS, 16):
                parts = [final[v, pl.ds((start + h * 8) * 8 + j, 8, stride=8), :] for h in range(2)]
                result[j, v, start : start + 16, :] = jnp.concatenate(parts, axis=0).astype(BF16)
        writes[v].start()

    for write in writes:
        write.wait()

    for step in range(GROUPS):
        to, _ = member_device(step)
        pairs = [(thick.at[1, 0], at_s.at[step]), (drift.at[0], ad_s.at[step]), (send_e.at[to], e_s.at[step])]
        pairs += [(send_c.at[v, to], c_s.at[v, step]) for v in range(FIELDS)]
        for src, sem in pairs:
            if step == 0:
                wait_sent(at_home, src, sem)
            else:
                settle(src, sem)
    wait_sent(obs_home, send_obs, ob_s.at[0])
    wait_sent(obs_home, index, ob_s.at[1])
    for side in range(2):
        settle(send_w.at[side], w_s.at[side])
        settle(obs.at[1], b_s.at[side, 8])
        settle(edge_send.at[side], n_s.at[side])
        for j in range(GROUPS):
            settle(thick.at[1, j], b_s.at[side, j])


def body(tiles, background, obs_value, obs_var, obs_index, ice_mask, wind_stress):
    dma = pltpu.SemaphoreType.DMA
    return pl.pallas_call(
        functools.partial(kernel, tiles),
        out_shape=jax.ShapeDtypeStruct(background.shape, BF16),
        in_specs=[pl.BlockSpec(memory_space=pltpu.HBM)] * 6,
        out_specs=pl.BlockSpec(memory_space=pltpu.HBM),
        scratch_shapes=[
            pltpu.VMEM(obs_value.shape, BF16),
            pltpu.VMEM(obs_var.shape, BF16),
            pltpu.VMEM(ice_mask.shape, jnp.int32),
            pltpu.VMEM(wind_stress.shape, BF16),
            pltpu.VMEM((3, ENS * RB, LANES), F32),
            pltpu.VMEM((16, LANES), BF16),
            pltpu.VMEM((3, GROUPS, 8, RB, LANES), BF16),
            pltpu.VMEM((GROUPS, 8, 2, RB, LANES), BF16),
            pltpu.VMEM((3, 16, LANES), BF16),
            pltpu.VMEM((PATCHES, obs_index.shape[2]), jnp.int32),
            pltpu.VMEM((3, PATCHES, RB, LANES), F32),
            pltpu.VMEM((PATCHES, RB, LANES), F32),
            pltpu.VMEM((80, CELLS), BF16),
            pltpu.VMEM((80, CELLS), BF16),
            pltpu.VMEM((WIDE, CELLS), BF16),
            pltpu.VMEM((WIDE, CELLS), BF16),
            pltpu.VMEM((80, WIDE), F32),
            pltpu.VMEM((WIDE, FIELDS * RB * LANES), BF16),
            pltpu.VMEM((2, ENS, LANES), F32),
            pltpu.VMEM((2, ENS, LANES), BF16),
            pltpu.VMEM((2, ENS, LANES), BF16),
            pltpu.VMEM((FIELDS, GROUPS, 64, LANES), BF16),
            pltpu.VMEM((FIELDS, (ROWS + 2 * EDGE_ROWS) * 8, LANES), BF16),
            pltpu.VMEM((GROUPS, 16, LANES), BF16),
            pltpu.VMEM((GROUPS, 16, LANES), BF16),
            pltpu.VMEM((2, RB, LANES), F32),
            pltpu.VMEM((2, RB, LANES), F32),
            pltpu.VMEM((ROWS + 16, LANES), F32),
            pltpu.VMEM((STRIP_ROWS + 16, LANES), F32),
            pltpu.VMEM((FIELDS, STRIP_ROWS * 8, LANES), F32),
            *[pltpu.VMEM((ROWS * 8, LANES), F32)] * 4,
            *[pltpu.VMEM(((ROWS + 2) * 8, LANES), F32)] * 5,
            *[pltpu.VMEM((STRIP_ROWS * 8, LANES), F32)] * 4,
            *[pltpu.VMEM(((STRIP_ROWS + 2) * 8, LANES), F32)] * 5,
            pltpu.VMEM((FIELDS, ROWS * 8, LANES), F32),
            pltpu.VMEM(background.shape, BF16),
            dma((4,)),
            dma((FIELDS,)),
            dma((GROUPS,)), dma((GROUPS,)),
            dma((GROUPS,)), dma((GROUPS,)),
            dma((2,)), dma((2,)),
            dma((2, 9)), dma((3, 9)),
            dma((2,)), dma((2,)),
            dma((FIELDS, GROUPS)), dma((FIELDS, GROUPS)),
            dma((GROUPS,)), dma((GROUPS,)),
            dma((2,)), dma((2,)),
        ],
        compiler_params=pltpu.CompilerParams(
            collective_id=0, has_side_effects=True, vmem_limit_bytes=60 * 1024 * 1024
        ),
        name="analysis_and_drift",
    )(background.reshape(8, FIELDS, GROUPS, RB, LANES), obs_value, obs_var, obs_index[0], ice_mask, wind_stress)


def solution(mesh):
    placed = (
        P("mem", None, None, "tile"),
        P("mem", "tile"),
        P("mem", "tile"),
        P("mem", "tile", None),
        P(None, "tile"),
        P(None, None, "tile"),
    )
    return jax.shard_map(
        functools.partial(body, mesh.shape["tile"]),
        mesh=mesh,
        in_specs=placed,
        out_specs=P("mem", None, None, "tile"),
        check_vma=False,
    )
```

time: 61.7 us -> 51.2 us (0.83)
  Pallas kernels: 56 us -> 49.3 us
  local copies, waits for them, and re-layouts: 5.32 us -> 1.77 us
    pallas_call x1, Pallas kernels: 56 us -> 49.3 us  [body(): pl.pallas_call(functools.partial(kernel, tiles), out_shape=jax.ShapeDtype...]
    unnamed x13 -> x1, local copies, waits for them, and re-layouts: 5.32 us -> 1.77 us
where the time goes in v2:
time: 51.2 us; the launch traced here: 51 us
  Pallas kernels  49.3 us (96%)
  local copies, waits for them, and re-layouts  1.77 us (3%)
    pallas_call x1, Pallas kernels, body(): pl.pallas_call(functools.partial(kernel, tiles), out_shape=jax.ShapeDtype...  49.3 us
    unnamed x1, local copies, waits for them, and re-layouts  1.77 us

profile of v2, /device:TPU:1, one launch (start us, length us, event | category | flops | bytes accessed | tf_op | source)
XLA Modules:
  0.0 51.0 jit_solution(10382929971751006023)
XLA Ops:
  0.0 49.3 %analysis_and_drift.1 = bf16[8,3,64,128]{3,2,1,0:T(8,128)(2,1)} custom-call(bf16[8,3,8,8,128]{4,3,2,1,0:T(8,128)(2,1)} %bitcast.2, bf16[8,128]{1,0:T(8,128)(2,1)} %obs_value_hbm.1, bf16[8,128]{1,0:T(8,128)(2,1)} %obs_var_hbm.1, s32[8,256]{1,0:T(8,128)} %bitcast.3, s32[64,128]{1,0:T(8,128)} %mask_hbm.1, bf16[2,64,128]{2,1,0:T(8,128)(2,1)} %wind_hbm.1), custom_call_target="tpu_custom_call" | custom-call | tf_op jit(solution)/shard_map/analysis_and_drift/pallas_call | solution.py:518
  49.3 1.8 %copy.8 = bf16[8,3,64,128]{3,2,1,0:T(8,128)(2,1)} copy(bf16[8,3,64,128]{3,2,1,0:T(8,128)(2,1)} %analysis_and_drift.1) | data formatting | bytes 786432

commit v3 on v2

v3 whole, which is shorter than its diff:
```python
import functools

import jax
import jax.numpy as jnp
from jax import lax
from jax.experimental import pallas as pl
from jax.experimental.pallas import tpu as pltpu
from jax.sharding import PartitionSpec as P

F32 = jnp.float32
BF16 = jnp.bfloat16
MESH = pl.DeviceIdType.MESH

ENS = 64
GROUPS = 8
RB = 8
ROWS = 64
PC = 16
W = 128
SPAN = PC + 2 * W
LANES = 128
PATCHES = 8
FIELDS = 3
NS_ITERS = 6
WIDE = PATCHES * ENS
CELLS = 3 * RB * LANES
HALO = 4
EDGE_ROWS = 4
STRIP_ROWS = 16 + 2 * EDGE_ROWS


def iota(shape, axis):
    return lax.broadcasted_iota(jnp.int32, shape, axis)


def aligned(start, size, by):
    return pl.ds(pl.multiple_of(start, by), size)


def split(x):
    high = x.astype(BF16)
    return high, (x - high.astype(F32)).astype(BF16)


def dot(a, b):
    return jnp.dot(a, b, preferred_element_type=F32)


def dot_lanes(a, b):
    return lax.dot_general(a, b, (((1,), (1,)), ((), ())), preferred_element_type=F32)


def block_diagonal(x):
    segment = iota(x.shape, 1) // ENS
    zero = jnp.zeros_like(x)
    return jnp.concatenate([jnp.where(segment == q, x, zero) for q in range(4)], axis=0)


def patch_products(left, right, left_parts=2, right_parts=2):
    rows = left.shape[0]
    left_high, left_low = split(left)
    right_high, right_low = split(right)
    out = []
    for half in range(2):
        lanes = slice(half * 256, (half + 1) * 256)
        main = block_diagonal(right_high[:, lanes])
        if left_parts == 2:
            both = dot(jnp.concatenate([left_high[:, lanes], left_low[:, lanes]], axis=0), main)
            total = both[:rows] + both[rows:]
        else:
            total = dot(left_high[:, lanes], main)
        if right_parts == 2:
            total = total + dot(left_high[:, lanes], block_diagonal(right_low[:, lanes]))
        out.append(total)
    return jnp.concatenate(out, axis=1)


def root_weights(system, projected):
    row = iota((ENS, WIDE), 0)
    eye = ((iota((ENS, WIDE), 1) % ENS) == row).astype(F32)
    full = system + (ENS - 1.0) * eye
    squares = jnp.sum(full * full, axis=0, keepdims=True)
    own = ((iota((PATCHES, WIDE), 1) // ENS) == iota((PATCHES, WIDE), 0)).astype(F32)
    norm = jnp.sum(own * squares, axis=1, keepdims=True)
    scale = jnp.sqrt(jnp.sum(own * norm, axis=0, keepdims=True))
    centring = eye - 1.0 / ENS
    iterate = (system + (ENS - 1.0) * centring) / scale
    inverse_root = centring
    for sweep in range(NS_ITERS):
        last = sweep == NS_ITERS - 1
        parts = 2 if last else 1
        product = patch_products(inverse_root, iterate, parts, parts) if sweep else iterate
        change = 0.5 * (eye - product)
        held = jnp.concatenate(([] if last else [iterate]) + [inverse_root, projected], axis=0)
        held = held + patch_products(held, change, 2, parts)
        if not last:
            iterate, held = held[:ENS], held[ENS:]
        inverse_root, projected = held[:ENS], held[ENS:]
    mean_weight = patch_products(projected, inverse_root)[:1] / scale
    return jnp.sqrt(ENS - 1.0) * (inverse_root / jnp.sqrt(scale)) + (mean_weight + 1.0 / ENS)


def kernel(
    tiles,
    prior, obs_value_hbm, obs_var_hbm, obs_index, mask_hbm, wind_hbm,
    out,
    obs_value, obs_var, ice_mask, wind,
    staged, tall, send_obs, thick, drift, obs, index,
    count, weight, anom_hi, anom_lo, pulls, heavy, acc, projected,
    masked, packed, edge_send, edge_recv,
    send_c, recv_c, send_e, recv_e,
    flat_rows, send_w, recv_w, padded, flat_halo, strip_halo,
    free, tau_x, tau_y, press, field_x, field_y, normal_x, normal_y, shear,
    strip_free, strip_tau_x, strip_tau_y, strip_press, strip_x, strip_y, strip_normal_x, strip_normal_y, strip_shear,
    final,
    in_s, at_s, at_r, ad_s, ad_r, ob_s, ob_r, b_s, b_r, n_s, n_r, c_s, c_r, e_s, e_r, w_s, w_r,
):
    me, tile = lax.axis_index("mem"), lax.axis_index("tile")
    core, z_lo = me % 2, me // 2
    half, ring = tile % 2, tile // 2
    z = half * 4 + z_lo

    def ring_device(at_z, at_core):
        return ((at_z % 4) * 2 + at_core, ring * 2 + at_z // 4)

    chip_mate = (me + 1 - 2 * core, tile)
    side_mate = (me + 1 - 2 * core, lax.rem(tile + tiles - 2 + 4 * core, tiles))

    loads = [
        pltpu.make_async_copy(src, dst, in_s.at[i])
        for i, (src, dst) in enumerate(
            (
                (prior.at[:, 0], staged.at[:, 0]),
                (obs_value_hbm, obs_value),
                (obs_var_hbm, obs_var),
                (mask_hbm, ice_mask),
                (wind_hbm, wind),
                (prior.at[:, pl.ds(1, 2)], staged.at[:, pl.ds(1, 2)]),
            )
        )
    ]
    for load in loads:
        load.start()

    barrier = pltpu.get_barrier_semaphore()

    def greet(step, carry):
        at = lax.rem(z * 2 + core + lax.rem(step + 7, 15) + 1, 16)
        pl.semaphore_signal(barrier, inc=1, device_id=ring_device(at // 2, at % 2), device_id_type=MESH)
        return carry

    lax.fori_loop(1, 16, greet, 0)
    pl.semaphore_signal(barrier, inc=1, device_id=side_mate, device_id_type=MESH)

    for load in loads:
        load.wait()
    flat_rows[0] = ice_mask[...].astype(F32)
    flat_rows[1] = wind[0].astype(F32)
    flat_rows[2] = wind[1].astype(F32)
    rows = pl.ds(pl.multiple_of(me * RB, RB), RB)
    surface = [obs_value[...].astype(F32), obs_var[...].astype(F32)]
    surface += [flat_rows[f, rows, :] for f in range(FIELDS)]
    send_obs[...] = jnp.concatenate(surface + [jnp.zeros((RB, LANES), F32)], axis=0).astype(BF16)

    pl.semaphore_wait(barrier, 16)

    def remote(src, dst, s_sem, r_sem, device):
        return pltpu.make_async_remote_copy(
            src_ref=src, dst_ref=dst, send_sem=s_sem, recv_sem=r_sem, device_id=device, device_id_type=MESH
        )

    def settle(ref, sem):
        pltpu.make_async_copy(ref, ref, sem).wait()

    def send_or_keep(same, src, dst, s_sem, r_sem, device):
        @pl.when(same)
        def _():
            pltpu.make_async_copy(src, dst, r_sem).start()

        @pl.when(jnp.logical_not(same))
        def _():
            remote(src, dst, s_sem, r_sem, device).start()

    def wait_sent(same, src, s_sem):
        @pl.when(jnp.logical_not(same))
        def _():
            settle(src, s_sem)

    owner = ring_device(me, half)
    obs_home = jnp.logical_and(owner[0] == me, owner[1] == tile)
    send_or_keep(obs_home, obs_index, index, ob_s.at[1], ob_r.at[1], owner)
    at_home = core == half
    far_first = (4, 3, 5, 2, 6, 1, 7, 0)
    for step in far_first:
        g = lax.rem(z + step, GROUPS)
        there = ring_device(g, half)
        if step:
            remote(staged.at[:, 0, g], thick.at[1, me], at_s.at[0], at_r.at[me], there).start()
        else:
            send_or_keep(at_home, staged.at[:, 0, g], thick.at[1, me], at_s.at[0], at_r.at[me], there)
    send_or_keep(obs_home, send_obs, obs.at[1], ob_s.at[0], ob_r.at[0], owner)
    mate_slot = 2 * core
    side_slot = 2 - 2 * core
    chips = (z_lo, z_lo + 1 - 2 * (z_lo % 2), z_lo + 2 - 4 * (z_lo // 2), 3 - z_lo)
    apart = (core + half) % 2

    def pass_on(i):
        chip = chips[i] * (1 - apart) + chips[3 - i] * apart
        for c in range(2):
            j = chip * 2 + c
            settle(thick.at[1, j], at_r.at[j])
            remote(thick.at[1, j], thick.at[side_slot, j], b_s.at[0], b_r.at[side_slot, 0], side_mate).start()
            remote(thick.at[1, j], thick.at[mate_slot, j], b_s.at[0], b_r.at[mate_slot, 0], chip_mate).start()

    for i in range(3):
        pass_on(i)

    settle(index, ob_r.at[1])
    cell = index[...].astype(F32)
    cell_row = jnp.floor((cell + 0.5) * (1.0 / SPAN))
    cell_col = cell - SPAN * cell_row
    row_at = iota((16, cell.shape[1]), 0).astype(F32)
    col_at = iota((3 * LANES, cell.shape[1]), 0).astype(F32)
    for p in range(PATCHES):
        rows = (row_at == cell_row[p : p + 1]).astype(F32).astype(BF16)
        cols = (col_at == cell_col[p : p + 1] + float(p * PC)).astype(F32).astype(BF16)
        hits = dot_lanes(rows, cols)
        for s in range(3):
            count[s, p] = hits[:RB, s * LANES : (s + 1) * LANES]

    settle(obs.at[1], ob_r.at[0])
    remote(obs.at[1], obs.at[side_slot], b_s.at[1], b_r.at[side_slot, 1], side_mate).start()
    remote(obs.at[1], obs.at[mate_slot], b_s.at[1], b_r.at[mate_slot, 1], chip_mate).start()
    pass_on(3)
    for step in far_first:
        g = lax.rem(z + step, GROUPS)
        there = ring_device(g, half)
        if step:
            remote(staged.at[:, pl.ds(1, 2), g], drift.at[me], ad_s.at[0], ad_r.at[0], there).start()
        else:
            send_or_keep(at_home, staged.at[:, pl.ds(1, 2), g], drift.at[me], ad_s.at[0], ad_r.at[0], there)

    def system_part(s, place):
        both = obs[s].astype(F32)
        values, variance = both[:RB], both[RB : 2 * RB]
        for p in range(PATCHES):
            weight[p * RB : (p + 1) * RB, :] = count[s, p] / variance
        tall[place] = thick[s].astype(F32).reshape(ENS * RB, LANES)

        def rows_pair(pair, carry):
            for h in range(2):
                r = pair * 2 + h
                x = tall[place, pl.ds(r, ENS, stride=RB), :]
                mean = jnp.sum(x, axis=0, keepdims=True) * (1.0 / ENS)
                anom = x - mean
                value = jnp.sum(jnp.where(iota((RB, LANES), 0) == r, values, 0.0), axis=0, keepdims=True)
                lanes = aligned((place * RB + r) * LANES, LANES, LANES)
                anom_hi[:, lanes], anom_lo[:, lanes] = split(anom)
                pull = weight[pl.ds(r, PATCHES, stride=RB), :] * (value - mean)
                pull_high = pull.astype(BF16).astype(F32)
                pulls[:, lanes] = jnp.concatenate([pull_high, pull - pull_high], axis=0).astype(BF16)
                for p in range(PATCHES):
                    heavy[p * ENS : (p + 1) * ENS, lanes] = (anom * weight[pl.ds(p * RB + r, 1), :]).astype(BF16)
            return carry

        lax.fori_loop(0, RB // 2, rows_pair, 0)
        span = slice(place * RB * LANES, (place + 1) * RB * LANES)
        main = dot_lanes(jnp.concatenate([anom_hi[:, span], anom_lo[:, span]], axis=0), heavy[:, span])
        part = main[:ENS] + main[ENS:]
        drawn = dot_lanes(pulls[:, span], anom_hi[:, span]) + dot_lanes(pulls[:, span], anom_lo[:, span])
        drawn = drawn[:PATCHES] + drawn[PATCHES:]
        if place == 0:
            acc[...] = part
            projected[...] = drawn
        else:
            acc[...] += part
            projected[...] += drawn

    system_part(1, 0)

    edge_lane = iota((ENS, LANES), 1)

    def spread(v):
        for r in range(RB):
            j = v * RB + r
            x = tall[v, pl.ds(r, ENS, stride=RB), :]
            here = (edge_lane // HALO) == j
            low = pltpu.roll(x, (HALO * j) % LANES, 1)
            high = pltpu.roll(x, (HALO * j + HALO) % LANES, 1)
            if j == 0:
                packed[0] = jnp.where(here, low, 0.0)
                packed[1] = jnp.where(here, high, 0.0)
            else:
                packed[0] = jnp.where(here, low, packed[0])
                packed[1] = jnp.where(here, high, packed[1])
            for p in range(PATCHES):
                masked[p * ENS : (p + 1) * ENS, j * LANES : (j + 1) * LANES] = jnp.where(
                    edge_lane // PC == p, x, 0.0
                ).astype(BF16)

    spread(0)

    def member_device(step):
        to = lax.rem(me + step, GROUPS)
        return to, (to, ring * 2 + core)

    for place, s in ((1, 2 - 2 * core), (2, 2 * core)):
        settle(obs.at[s], b_r.at[s, 1])
        if place == 2:
            sides = []
            for side, first in ((0, LANES - HALO), (2, 0)):
                surface = obs[side].astype(F32)
                total = jnp.zeros((RB, LANES), F32)
                for f in range(FIELDS):
                    at = (f * GROUPS + z) * HALO
                    moved = pltpu.roll(surface[(f + 2) * RB : (f + 3) * RB], lax.rem(at - first + LANES, LANES), 1)
                    spot = iota((RB, LANES), 1) // HALO == f * GROUPS + z
                    total = jnp.where(spot, moved, total)
                sides.append(total)
            send_w[...] = jnp.concatenate(sides, axis=0).astype(BF16)
            for step in far_first:
                to, there = member_device(step)
                if step:
                    remote(send_w, recv_w.at[z], w_s.at[0], w_r.at[0], there).start()
                else:
                    send_or_keep(at_home, send_w, recv_w.at[z], w_s.at[0], w_r.at[0], there)
        settle(thick.at[s], b_r.at[s, 0])
        system_part(s, place)

    own_lanes = iota((PATCHES, WIDE), 1) // ENS == iota((PATCHES, WIDE), 0)
    drawn = jnp.where(own_lanes, jnp.concatenate([projected[...]] * PATCHES, axis=1), 0.0)
    drawn = jnp.broadcast_to(jnp.sum(drawn, axis=0, keepdims=True), (16, WIDE))
    weights = root_weights(acc[...], drawn)
    left = jnp.concatenate(split(weights), axis=0)

    for v in range(FIELDS):
        if v == 1:
            settle(drift, ad_r.at[0])
            for f in (1, 2):
                tall[f] = drift[:, :, f - 1].astype(F32).reshape(ENS * RB, LANES)
                spread(f)
            for side, p in ((0, 0), (1, PATCHES - 1)):
                edge = dot(left[:, p * ENS : (p + 1) * ENS], packed[side].astype(BF16))
                edge_send[side] = (edge[:ENS] + edge[ENS:]).astype(BF16)
            remote(edge_send.at[1 - core], edge_recv.at[core], n_s.at[0], n_r.at[0], chip_mate).start()
            remote(edge_send.at[core], edge_recv.at[1 - core], n_s.at[0], n_r.at[0], side_mate).start()
        for pair in range(RB // 2):
            at = (v * RB + pair * 2) * LANES
            got = dot(left, masked[:, at : at + 256])
            got = got[:ENS] + got[ENS:]
            for to in range(GROUPS):
                rows = slice(to * 8, to * 8 + 8)
                send_c[v, to, pair * 16 : pair * 16 + 16, :] = jnp.concatenate(
                    [got[rows, :LANES], got[rows, LANES:]], axis=0
                ).astype(BF16)
        for step in far_first:
            to, there = member_device(step)
            if step:
                remote(send_c.at[v, to], recv_c.at[v, aligned(EDGE_ROWS * 8 + z * 64, 64, 16)], c_s.at[0], c_r.at[v], there).start()
            else:
                send_or_keep(at_home, send_c.at[v, to], recv_c.at[v, aligned(EDGE_ROWS * 8 + z * 64, 64, 16)], c_s.at[0], c_r.at[v], there)
    at_lane = iota((8, LANES), 1)
    lane_group, lane_in = at_lane // 32, at_lane % 32
    is_right = jnp.logical_and(lane_in >= 8, lane_in < 12)
    is_left = jnp.logical_and(lane_in >= 12, lane_in < 16)

    def strip_edges(from_left, from_right, j, q):
        left_part = pltpu.roll(from_left, (32 * q + 12 - HALO * j) % LANES, 1)
        right_part = pltpu.roll(from_right, (32 * q + 8 - HALO * j) % LANES, 1)
        here = lane_group == q
        part = jnp.where(jnp.logical_and(here, is_left), left_part, 0.0)
        return jnp.where(jnp.logical_and(here, is_right), right_part, part)

    pick_row, pick_lane = iota((4 * LANES, LANES), 0), iota((4 * LANES, LANES), 1)
    pick_col, pick_in = pick_row % LANES, pick_lane % 32
    wanted = jnp.where(pick_in < 8, 120 + pick_in, jnp.where(jnp.logical_and(pick_in >= 16, pick_in < 24), pick_in - 16, -1))
    picks = jnp.logical_and(pick_row // LANES == pick_lane // 32, pick_col == wanted).astype(F32).astype(BF16)

    none = jnp.zeros((8, LANES), F32)
    for ref in (field_x, field_y, normal_x, normal_y, shear):
        ref[0:8, :] = none
        ref[(ROWS + 1) * 8 :, :] = none
    for ref in (strip_x, strip_y, strip_normal_x, strip_normal_y, strip_shear):
        ref[0:8, :] = none
        ref[(STRIP_ROWS + 1) * 8 :, :] = none
    for v in range(FIELDS):
        recv_c[v, 0 : EDGE_ROWS * 8, :] = jnp.zeros((EDGE_ROWS * 8, LANES), BF16)
        recv_c[v, (EDGE_ROWS + ROWS) * 8 :, :] = jnp.zeros((EDGE_ROWS * 8, LANES), BF16)

    settle(edge_recv, n_r.at[0])
    for to in range(GROUPS):
        rows = slice(to * 8, to * 8 + 8)
        send_e[to] = jnp.concatenate(
            [edge_recv[0].astype(F32)[rows], edge_recv[1].astype(F32)[rows]], axis=0
        ).astype(BF16)
    for step in far_first:
        to, there = member_device(step)
        if step:
            remote(send_e.at[to], recv_e.at[z], e_s.at[0], e_r.at[0], there).start()
        else:
            send_or_keep(at_home, send_e.at[to], recv_e.at[z], e_s.at[0], e_r.at[0], there)

    settle(recv_w, w_r.at[0])
    edges = jnp.sum(recv_w[...].astype(F32), axis=0)
    for f, (ref, strip_ref) in enumerate(((free, strip_free), (tau_x, strip_tau_x), (tau_y, strip_tau_y))):
        gain = 1.0 / 1.5 if f == 0 else 0.5
        whole = flat_rows[f]
        for row in range(ROWS):
            ref[row * 8 : row * 8 + 8, :] = jnp.broadcast_to(whole[row : row + 1] * gain, (8, LANES))
        padded[0:8, :] = jnp.zeros((8, LANES), F32)
        padded[8 + ROWS :, :] = jnp.zeros((8, LANES), F32)
        padded[8 : 8 + ROWS, :] = whole
        parts = [padded[4 + 16 * q : 4 + 16 * q + STRIP_ROWS, :].astype(BF16) for q in range(4)]
        own = dot(jnp.concatenate(parts, axis=1), picks)
        flat_halo[...] = jnp.zeros(flat_halo.shape, F32)
        for q in range(4):
            for g in range(max(0, 2 * q - 1), min(GROUPS, 2 * q + 3)):
                start = 8 + 8 * g - 16 * q + EDGE_ROWS
                flat_halo[start : start + 8, :] += strip_edges(edges[:RB], edges[RB:], f * GROUPS + g, q)
        whole = (own + flat_halo[8 : 8 + STRIP_ROWS, :]) * gain
        for row in range(STRIP_ROWS):
            strip_ref[row * 8 : row * 8 + 8, :] = jnp.broadcast_to(whole[row : row + 1], (8, LANES))

    def pressure(x):
        return 0.125 * (jnp.maximum(x, 0.0) + jnp.log1p(jnp.exp(-jnp.abs(x))))

    def unpack(v):
        settle(recv_c.at[v, pl.ds(EDGE_ROWS * 8, ROWS * 8)], c_r.at[v])
        main = recv_c[v, EDGE_ROWS * 8 : (EDGE_ROWS + ROWS) * 8, :].astype(F32)
        if v == 0:
            press[...] = pressure(main)
            final[0] = main
        else:
            (field_x, field_y)[v - 1][8 : 8 + ROWS * 8, :] = main

    def write_out(v):
        for j in range(GROUPS):
            for start in range(0, ROWS, 16):
                parts = [final[v, pl.ds((start + h * 8) * 8 + j, 8, stride=8), :] for h in range(2)]
                out[j, v, start : start + 16, :] = jnp.concatenate(parts, axis=0).astype(BF16)

    unpack(0)
    write_out(0)
    unpack(1)
    settle(recv_e, e_r.at[0])
    for row in range(STRIP_ROWS):
        for v in range(FIELDS):
            total = none
            for q in range(4):
                at = 16 * q - EDGE_ROWS + row
                if 0 <= at < ROWS:
                    edges = recv_e[at // RB].astype(F32)
                    total = total + strip_edges(edges[:8], edges[8:], v * RB + at % RB, q)
            strip_halo[v, row * 8 : row * 8 + 8, :] = total
    unpack(2)

    strip_rows = STRIP_ROWS * 8
    for v in range(FIELDS):
        parts = [recv_c[v, 128 * q : 128 * q + strip_rows, :] for q in range(4)]
        strip = dot(jnp.concatenate(parts, axis=1), picks) + strip_halo[v]
        if v == 0:
            row = iota((strip_rows, LANES), 0) // 8
            group = iota((strip_rows, LANES), 1) // 32
            outside = jnp.logical_or(
                jnp.logical_and(group == 0, row < EDGE_ROWS), jnp.logical_and(group == 3, row >= STRIP_ROWS - EDGE_ROWS)
            )
            strip_press[...] = jnp.where(outside, 0.0, pressure(strip))
        else:
            (strip_x, strip_y)[v - 1][8 : 8 + strip_rows, :] = strip

    def difference(x):
        return pltpu.roll(x, LANES - 1, 1) - pltpu.roll(x, 1, 1)

    main_refs = (field_x, field_y, normal_x, normal_y, shear, press, free, tau_x, tau_y)
    strip_refs = (
        strip_x, strip_y, strip_normal_x, strip_normal_y, strip_shear, strip_press, strip_free, strip_tau_x, strip_tau_y,
    )
    height = 64
    blocks = [(main_refs, i) for i in range(ROWS * 8 // height)]
    for i in range(strip_rows // height):
        blocks.insert(3 * i + 2, (strip_refs, i))

    for sweep in range(2):
        for refs, i in blocks:
            f_x, f_y, n_x, n_y, s_xy, p_ref = refs[:6]
            up, here, down = (slice(i * height + 8 * k, (i + 1) * height + 8 * k) for k in range(3))
            across_x, across_y = difference(f_x[here, :]), difference(f_y[here, :])
            along_x = f_x[down, :] - f_x[up, :]
            along_y = f_y[down, :] - f_y[up, :]
            p = p_ref[up, :]
            spread = across_x + along_y - 1.0
            skew = 0.25 * (across_x - along_y)
            new = (p * (spread + skew), p * (spread - skew), (0.5 * p) * (along_x + across_y))
            for ref, term in zip((n_x, n_y, s_xy), new):
                ref[here, :] = term if sweep == 0 else 0.5 * ref[here, :] + term
        for refs, i in blocks:
            f_x, f_y, n_x, n_y, s_xy, _, open_ref, t_x, t_y = refs
            up, here, down = (slice(i * height + 8 * k, (i + 1) * height + 8 * k) for k in range(3))
            force_x = difference(n_x[here, :]) + (s_xy[down, :] - s_xy[up, :])
            force_y = difference(s_xy[here, :]) + (n_y[down, :] - n_y[up, :])
            f_x[here, :] = open_ref[up, :] * (f_x[here, :] + t_x[up, :] + 0.25 * force_x)
            f_y[here, :] = open_ref[up, :] * (f_y[here, :] + t_y[up, :] + 0.25 * force_y)

    for v, (ref, strip_ref) in ((1, (field_x, strip_x)), (2, (field_y, strip_y))):
        for row in range(0, ROWS, 4):
            q, at = row // 16, row % 16 + EDGE_ROWS + 1
            main = ref[(row + 1) * 8 : (row + 5) * 8, :]
            edge = strip_ref[at * 8 : at * 8 + 32, :]
            col = iota((32, LANES), 1)
            main = jnp.where(col < HALO, pltpu.roll(edge, (LANES - 32 * q - 16) % LANES, 1), main)
            main = jnp.where(col >= LANES - HALO, pltpu.roll(edge, (120 - 32 * q) % LANES, 1), main)
            final[v, row * 8 : row * 8 + 32, :] = main
        write_out(v)

    settle(thick.at[pl.ds(0, 2)], b_s.at[0])
    settle(obs.at[pl.ds(0, 2)], b_s.at[1])
    settle(edge_send, n_s.at[0])
    for sent, sem in ((thick.at[1], at_s), (drift, ad_s), (recv_e, e_s), (recv_w, w_s)):

        @pl.when(at_home)
        def _():
            settle(sent.at[pl.ds(0, GROUPS - 1)], sem.at[0])

        @pl.when(jnp.logical_not(at_home))
        def _():
            settle(sent, sem.at[0])

    @pl.when(at_home)
    def _():
        settle(send_c.at[:, pl.ds(0, GROUPS - 1)], c_s.at[0])

    @pl.when(jnp.logical_not(at_home))
    def _():
        settle(send_c, c_s.at[0])

    wait_sent(obs_home, send_obs, ob_s.at[0])
    wait_sent(obs_home, index, ob_s.at[1])


def body(tiles, background, obs_value, obs_var, obs_index, ice_mask, wind_stress):
    dma = pltpu.SemaphoreType.DMA
    inputs = (background.reshape(8, FIELDS, GROUPS, RB, LANES), obs_value, obs_var, obs_index[0], ice_mask, wind_stress)
    return pl.pallas_call(
        functools.partial(kernel, tiles),
        out_shape=jax.ShapeDtypeStruct(background.shape, BF16),
        in_specs=[pl.BlockSpec(memory_space=pltpu.HBM)] * 6,
        out_specs=pl.BlockSpec(memory_space=pltpu.VMEM),
        scratch_shapes=[
            pltpu.VMEM(obs_value.shape, BF16),
            pltpu.VMEM(obs_var.shape, BF16),
            pltpu.VMEM(ice_mask.shape, jnp.int32),
            pltpu.VMEM(wind_stress.shape, BF16),
            pltpu.VMEM((8, FIELDS, GROUPS, RB, LANES), BF16),
            pltpu.VMEM((3, ENS * RB, LANES), F32),
            pltpu.VMEM((48, LANES), BF16),
            pltpu.VMEM((3, GROUPS, 8, RB, LANES), BF16),
            pltpu.VMEM((GROUPS, 8, 2, RB, LANES), BF16),
            pltpu.VMEM((3, 48, LANES), BF16),
            pltpu.VMEM((PATCHES, obs_index.shape[2]), jnp.int32),
            pltpu.VMEM((3, PATCHES, RB, LANES), F32),
            pltpu.VMEM((PATCHES * RB, LANES), F32),
            pltpu.VMEM((ENS, CELLS), BF16),
            pltpu.VMEM((ENS, CELLS), BF16),
            pltpu.VMEM((16, CELLS), BF16),
            pltpu.VMEM((WIDE, CELLS), BF16),
            pltpu.VMEM((ENS, WIDE), F32),
            pltpu.VMEM((PATCHES, ENS), F32),
            pltpu.VMEM((WIDE, FIELDS * RB * LANES), BF16),
            pltpu.VMEM((2, ENS, LANES), F32),
            pltpu.VMEM((2, ENS, LANES), BF16),
            pltpu.VMEM((2, ENS, LANES), BF16),
            pltpu.VMEM((FIELDS, GROUPS, 64, LANES), BF16),
            pltpu.VMEM((FIELDS, (ROWS + 2 * EDGE_ROWS) * 8, LANES), BF16),
            pltpu.VMEM((GROUPS, 16, LANES), BF16),
            pltpu.VMEM((GROUPS, 16, LANES), BF16),
            pltpu.VMEM((FIELDS, ROWS, LANES), F32),
            pltpu.VMEM((16, LANES), BF16),
            pltpu.VMEM((GROUPS, 16, LANES), BF16),
            pltpu.VMEM((ROWS + 16, LANES), F32),
            pltpu.VMEM((STRIP_ROWS + 16, LANES), F32),
            pltpu.VMEM((FIELDS, STRIP_ROWS * 8, LANES), F32),
            *[pltpu.VMEM((ROWS * 8, LANES), F32)] * 4,
            *[pltpu.VMEM(((ROWS + 2) * 8, LANES), F32)] * 5,
            *[pltpu.VMEM((STRIP_ROWS * 8, LANES), F32)] * 4,
            *[pltpu.VMEM(((STRIP_ROWS + 2) * 8, LANES), F32)] * 5,
            pltpu.VMEM((FIELDS, ROWS * 8, LANES), F32),
            dma((6,)),
            dma((1,)), dma((GROUPS,)),
            dma((1,)), dma((1,)),
            dma((2,)), dma((2,)),
            dma((2,)), dma((3, 2)),
            dma((1,)), dma((1,)),
            dma((1,)), dma((FIELDS,)),
            dma((1,)), dma((1,)),
            dma((1,)), dma((1,)),
        ],
        compiler_params=pltpu.CompilerParams(
            collective_id=0, has_side_effects=True, vmem_limit_bytes=50 * 1024 * 1024
        ),
        name="analysis_and_drift",
    )(*[pltpu.with_memory_space_constraint(x, pltpu.HBM) for x in inputs])


def solution(mesh):
    placed = (
        P("mem", None, None, "tile"),
        P("mem", "tile"),
        P("mem", "tile"),
        P("mem", "tile", None),
        P(None, "tile"),
        P(None, None, "tile"),
    )
    return jax.shard_map(
        functools.partial(body, mesh.shape["tile"]),
        mesh=mesh,
        in_specs=placed,
        out_specs=P("mem", None, None, "tile"),
        check_vma=False,
    )
```

time: 51.2 us -> 42.5 us (0.83)
  Pallas kernels: 49.3 us -> 41.6 us
  local copies, waits for them, and re-layouts: 1.77 us -> 0.75 us
    pallas_call x1, Pallas kernels: 49.3 us -> 41.6 us  [body(): pl.pallas_call(functools.partial(kernel, tiles), out_shape=jax.ShapeDtype...]
    unnamed x1, local copies, waits for them, and re-layouts: 1.77 us -> 0.75 us
where the time goes in v3:
time: 42.5 us; the launch traced here: 42.3 us
  Pallas kernels  41.6 us (98%)
  local copies, waits for them, and re-layouts  0.75 us (2%)
    pallas_call x1, Pallas kernels, body(): pl.pallas_call(functools.partial(kernel, tiles), out_shape=jax.ShapeDtype...  41.6 us

profile of v3, /device:TPU:1, one launch (start us, length us, event | category | flops | bytes accessed | tf_op | source)
XLA Modules:
  0.0 42.3 jit_solution(13503573532746916814)
XLA Ops:
  0.0 41.6 %analysis_and_drift.1 = bf16[8,3,64,128]{3,2,1,0:T(8,128)(2,1)S(1)} custom-call(bf16[8,3,8,8,128]{4,3,2,1,0:T(8,128)(2,1)} %bitcast.2, bf16[8,128]{1,0:T(8,128)(2,1)} %obs_value_hbm.1, bf16[8,128]{1,0:T(8,128)(2,1)} %obs_var_hbm.1, s32[8,256]{1,0:T(8,128)} %bitcast.3, s32[64,128]{1,0:T(8,128)} %mask_hbm.1, bf16[2,64,128]{2,1,0:T(8,128)(2,1)} %wind_hbm.1), custom_call_target="tpu_custom_call" | custom-call | tf_op jit(solution)/shard_map/analysis_and_drift/pallas_call | solution.py:543
  41.6 0.7 %copy.8 = bf16[8,3,64,128]{3,2,1,0:T(8,128)(2,1)} copy(bf16[8,3,64,128]{3,2,1,0:T(8,128)(2,1)S(1)} %analysis_and_drift.1) | data formatting | bytes 786432

commit v4 on v3

--- a/solution.py
+++ b/solution.py
@@ -56,21 +56,21 @@
     return jnp.concatenate([jnp.where(segment == q, x, zero) for q in range(4)], axis=0)
 
 
-def patch_products(left, right, left_parts=2, right_parts=2):
+def patch_blocks(right, parts):
+    lanes = [slice(half * 256, (half + 1) * 256) for half in range(2)]
+    return [[block_diagonal(part[:, at]) for part in split(right)[:parts]] for at in lanes]
+
+
+def patch_products(left, blocks):
     rows = left.shape[0]
     left_high, left_low = split(left)
-    right_high, right_low = split(right)
     out = []
-    for half in range(2):
+    for half, parts in enumerate(blocks):
         lanes = slice(half * 256, (half + 1) * 256)
-        main = block_diagonal(right_high[:, lanes])
-        if left_parts == 2:
-            both = dot(jnp.concatenate([left_high[:, lanes], left_low[:, lanes]], axis=0), main)
-            total = both[:rows] + both[rows:]
-        else:
-            total = dot(left_high[:, lanes], main)
-        if right_parts == 2:
-            total = total + dot(left_high[:, lanes], block_diagonal(right_low[:, lanes]))
+        both = dot(jnp.concatenate([left_high[:, lanes], left_low[:, lanes]], axis=0), parts[0])
+        total = both[:rows] + both[rows:]
+        if len(parts) == 2:
+            total = total + dot(left_high[:, lanes], parts[1])
         out.append(total)
     return jnp.concatenate(out, axis=1)
 
@@ -84,19 +84,18 @@
     norm = jnp.sum(own * squares, axis=1, keepdims=True)
     scale = jnp.sqrt(jnp.sum(own * norm, axis=0, keepdims=True))
     centring = eye - 1.0 / ENS
-    iterate = (system + (ENS - 1.0) * centring) / scale
+    product = (system + (ENS - 1.0) * centring) / scale
     inverse_root = centring
     for sweep in range(NS_ITERS):
         last = sweep == NS_ITERS - 1
-        parts = 2 if last else 1
-        product = patch_products(inverse_root, iterate, parts, parts) if sweep else iterate
-        change = 0.5 * (eye - product)
-        held = jnp.concatenate(([] if last else [iterate]) + [inverse_root, projected], axis=0)
-        held = held + patch_products(held, change, 2, parts)
+        blocks = patch_blocks(0.5 * (eye - product), 2 if last else 1)
+        held = jnp.concatenate(([] if last else [product]) + [inverse_root, projected], axis=0)
+        held = held + patch_products(held, blocks)
         if not last:
-            iterate, held = held[:ENS], held[ENS:]
+            product, held = held[:ENS], held[ENS:]
+            product = product + patch_products(product, blocks)
         inverse_root, projected = held[:ENS], held[ENS:]
-    mean_weight = patch_products(projected, inverse_root)[:1] / scale
+    mean_weight = patch_products(projected, patch_blocks(inverse_root, 2))[:1] / scale
     return jnp.sqrt(ENS - 1.0) * (inverse_root / jnp.sqrt(scale)) + (mean_weight + 1.0 / ENS)
 
 
@@ -106,14 +105,14 @@
     out,
     obs_value, obs_var, ice_mask, wind,
     staged, tall, send_obs, thick, drift, obs, index,
-    count, weight, anom_hi, anom_lo, pulls, heavy, acc, projected,
+    count, weight, anom_hi, anom_lo, pulls, heavy, heavy_lo, acc, projected,
     masked, packed, edge_send, edge_recv,
     send_c, recv_c, send_e, recv_e,
-    flat_rows, send_w, recv_w, padded, flat_halo, strip_halo,
+    flat_rows, padded, flat_own, flat_halo, strip_halo,
     free, tau_x, tau_y, press, field_x, field_y, normal_x, normal_y, shear,
     strip_free, strip_tau_x, strip_tau_y, strip_press, strip_x, strip_y, strip_normal_x, strip_normal_y, strip_shear,
     final,
-    in_s, at_s, at_r, ad_s, ad_r, ob_s, ob_r, b_s, b_r, n_s, n_r, c_s, c_r, e_s, e_r, w_s, w_r,
+    in_s, at_s, at_r, ad_s, ad_r, ob_s, ob_r, b_s, b_r, n_s, n_r, c_s, c_r, e_s, e_r,
 ):
     me, tile = lax.axis_index("mem"), lax.axis_index("tile")
     core, z_lo = me % 2, me // 2
@@ -212,8 +211,8 @@
             remote(thick.at[1, j], thick.at[side_slot, j], b_s.at[0], b_r.at[side_slot, 0], side_mate).start()
             remote(thick.at[1, j], thick.at[mate_slot, j], b_s.at[0], b_r.at[mate_slot, 0], chip_mate).start()
 
-    for i in range(3):
-        pass_on(i)
+    pass_on(0)
+    pass_on(1)
 
     settle(index, ob_r.at[1])
     cell = index[...].astype(F32)
@@ -228,6 +227,7 @@
         for s in range(3):
             count[s, p] = hits[:RB, s * LANES : (s + 1) * LANES]
 
+    pass_on(2)
     settle(obs.at[1], ob_r.at[0])
     remote(obs.at[1], obs.at[side_slot], b_s.at[1], b_r.at[side_slot, 1], side_mate).start()
     remote(obs.at[1], obs.at[mate_slot], b_s.at[1], b_r.at[mate_slot, 1], chip_mate).start()
@@ -247,34 +247,35 @@
             weight[p * RB : (p + 1) * RB, :] = count[s, p] / variance
         tall[place] = thick[s].astype(F32).reshape(ENS * RB, LANES)
 
-        def rows_pair(pair, carry):
+        for pair in range(RB // 2):
             for h in range(2):
                 r = pair * 2 + h
                 x = tall[place, pl.ds(r, ENS, stride=RB), :]
                 mean = jnp.sum(x, axis=0, keepdims=True) * (1.0 / ENS)
                 anom = x - mean
-                value = jnp.sum(jnp.where(iota((RB, LANES), 0) == r, values, 0.0), axis=0, keepdims=True)
-                lanes = aligned((place * RB + r) * LANES, LANES, LANES)
+                at = (place * RB + r) * LANES
+                lanes = slice(at, at + LANES)
                 anom_hi[:, lanes], anom_lo[:, lanes] = split(anom)
-                pull = weight[pl.ds(r, PATCHES, stride=RB), :] * (value - mean)
+                pull = weight[pl.ds(r, PATCHES, stride=RB), :] * (values[r : r + 1] - mean)
                 pull_high = pull.astype(BF16).astype(F32)
                 pulls[:, lanes] = jnp.concatenate([pull_high, pull - pull_high], axis=0).astype(BF16)
                 for p in range(PATCHES):
-                    heavy[p * ENS : (p + 1) * ENS, lanes] = (anom * weight[pl.ds(p * RB + r, 1), :]).astype(BF16)
-            return carry
-
-        lax.fori_loop(0, RB // 2, rows_pair, 0)
-        span = slice(place * RB * LANES, (place + 1) * RB * LANES)
-        main = dot_lanes(jnp.concatenate([anom_hi[:, span], anom_lo[:, span]], axis=0), heavy[:, span])
-        part = main[:ENS] + main[ENS:]
-        drawn = dot_lanes(pulls[:, span], anom_hi[:, span]) + dot_lanes(pulls[:, span], anom_lo[:, span])
-        drawn = drawn[:PATCHES] + drawn[PATCHES:]
-        if place == 0:
-            acc[...] = part
-            projected[...] = drawn
-        else:
-            acc[...] += part
-            projected[...] += drawn
+                    row = p * RB + r
+                    high, low = split(anom * weight[row : row + 1, :])
+                    heavy[p * ENS : (p + 1) * ENS, lanes] = high
+                    heavy_lo[p * ENS : (p + 1) * ENS, lanes] = low
+            at = (place * RB + pair * 2) * LANES
+            span = slice(at, at + 2 * LANES)
+            main = dot_lanes(jnp.concatenate([anom_hi[:, span], anom_lo[:, span]], axis=0), heavy[:, span])
+            part = main[:ENS] + main[ENS:] + dot_lanes(anom_hi[:, span], heavy_lo[:, span])
+            drawn = dot_lanes(pulls[:, span], anom_hi[:, span]) + dot_lanes(pulls[:, span], anom_lo[:, span])
+            drawn = drawn[:PATCHES] + drawn[PATCHES:]
+            if place == 0 and pair == 0:
+                acc[...] = part
+                projected[...] = drawn
+            else:
+                acc[...] += part
+                projected[...] += drawn
 
     system_part(1, 0)
 
@@ -284,15 +285,11 @@
         for r in range(RB):
             j = v * RB + r
             x = tall[v, pl.ds(r, ENS, stride=RB), :]
-            here = (edge_lane // HALO) == j
-            low = pltpu.roll(x, (HALO * j) % LANES, 1)
-            high = pltpu.roll(x, (HALO * j + HALO) % LANES, 1)
-            if j == 0:
-                packed[0] = jnp.where(here, low, 0.0)
-                packed[1] = jnp.where(here, high, 0.0)
-            else:
-                packed[0] = jnp.where(here, low, packed[0])
-                packed[1] = jnp.where(here, high, packed[1])
+            part, at = j // 16, j % 16
+            for side, shift in ((0, 8 * at), (1, 8 * at + 8)):
+                moved = pltpu.roll(x, shift % LANES, 1)
+                held = packed[side, part] if at else 0.0
+                packed[side, part] = jnp.where(edge_lane // HALO == 2 * at + side, moved, held)
             for p in range(PATCHES):
                 masked[p * ENS : (p + 1) * ENS, j * LANES : (j + 1) * LANES] = jnp.where(
                     edge_lane // PC == p, x, 0.0
@@ -306,24 +303,6 @@
 
     for place, s in ((1, 2 - 2 * core), (2, 2 * core)):
         settle(obs.at[s], b_r.at[s, 1])
-        if place == 2:
-            sides = []
-            for side, first in ((0, LANES - HALO), (2, 0)):
-                surface = obs[side].astype(F32)
-                total = jnp.zeros((RB, LANES), F32)
-                for f in range(FIELDS):
-                    at = (f * GROUPS + z) * HALO
-                    moved = pltpu.roll(surface[(f + 2) * RB : (f + 3) * RB], lax.rem(at - first + LANES, LANES), 1)
-                    spot = iota((RB, LANES), 1) // HALO == f * GROUPS + z
-                    total = jnp.where(spot, moved, total)
-                sides.append(total)
-            send_w[...] = jnp.concatenate(sides, axis=0).astype(BF16)
-            for step in far_first:
-                to, there = member_device(step)
-                if step:
-                    remote(send_w, recv_w.at[z], w_s.at[0], w_r.at[0], there).start()
-                else:
-                    send_or_keep(at_home, send_w, recv_w.at[z], w_s.at[0], w_r.at[0], there)
         settle(thick.at[s], b_r.at[s, 0])
         system_part(s, place)
 
@@ -340,7 +319,7 @@
                 tall[f] = drift[:, :, f - 1].astype(F32).reshape(ENS * RB, LANES)
                 spread(f)
             for side, p in ((0, 0), (1, PATCHES - 1)):
-                edge = dot(left[:, p * ENS : (p + 1) * ENS], packed[side].astype(BF16))
+                edge = dot(left[:, p * ENS : (p + 1) * ENS], jnp.concatenate([packed[side, 0], packed[side, 1]], axis=1).astype(BF16))
                 edge_send[side] = (edge[:ENS] + edge[ENS:]).astype(BF16)
             remote(edge_send.at[1 - core], edge_recv.at[core], n_s.at[0], n_r.at[0], chip_mate).start()
             remote(edge_send.at[core], edge_recv.at[1 - core], n_s.at[0], n_r.at[0], side_mate).start()
@@ -360,16 +339,9 @@
             else:
                 send_or_keep(at_home, send_c.at[v, to], recv_c.at[v, aligned(EDGE_ROWS * 8 + z * 64, 64, 16)], c_s.at[0], c_r.at[v], there)
     at_lane = iota((8, LANES), 1)
-    lane_group, lane_in = at_lane // 32, at_lane % 32
-    is_right = jnp.logical_and(lane_in >= 8, lane_in < 12)
-    is_left = jnp.logical_and(lane_in >= 12, lane_in < 16)
-
-    def strip_edges(from_left, from_right, j, q):
-        left_part = pltpu.roll(from_left, (32 * q + 12 - HALO * j) % LANES, 1)
-        right_part = pltpu.roll(from_right, (32 * q + 8 - HALO * j) % LANES, 1)
-        here = lane_group == q
-        part = jnp.where(jnp.logical_and(here, is_left), left_part, 0.0)
-        return jnp.where(jnp.logical_and(here, is_right), right_part, part)
+
+    def strip_edges(part, at, q):
+        return jnp.where(at_lane // 8 == 4 * q + 1, pltpu.roll(part, (32 * q + 8 - 8 * at) % LANES, 1), 0.0)
 
     pick_row, pick_lane = iota((4 * LANES, LANES), 0), iota((4 * LANES, LANES), 1)
     pick_col, pick_in = pick_row % LANES, pick_lane % 32
@@ -387,23 +359,7 @@
         recv_c[v, 0 : EDGE_ROWS * 8, :] = jnp.zeros((EDGE_ROWS * 8, LANES), BF16)
         recv_c[v, (EDGE_ROWS + ROWS) * 8 :, :] = jnp.zeros((EDGE_ROWS * 8, LANES), BF16)
 
-    settle(edge_recv, n_r.at[0])
-    for to in range(GROUPS):
-        rows = slice(to * 8, to * 8 + 8)
-        send_e[to] = jnp.concatenate(
-            [edge_recv[0].astype(F32)[rows], edge_recv[1].astype(F32)[rows]], axis=0
-        ).astype(BF16)
-    for step in far_first:
-        to, there = member_device(step)
-        if step:
-            remote(send_e.at[to], recv_e.at[z], e_s.at[0], e_r.at[0], there).start()
-        else:
-            send_or_keep(at_home, send_e.at[to], recv_e.at[z], e_s.at[0], e_r.at[0], there)
-
-    settle(recv_w, w_r.at[0])
-    edges = jnp.sum(recv_w[...].astype(F32), axis=0)
-    for f, (ref, strip_ref) in enumerate(((free, strip_free), (tau_x, strip_tau_x), (tau_y, strip_tau_y))):
-        gain = 1.0 / 1.5 if f == 0 else 0.5
+    for f, (ref, gain) in enumerate(((free, 1.0 / 1.5), (tau_x, 0.5), (tau_y, 0.5))):
         whole = flat_rows[f]
         for row in range(ROWS):
             ref[row * 8 : row * 8 + 8, :] = jnp.broadcast_to(whole[row : row + 1] * gain, (8, LANES))
@@ -411,15 +367,25 @@
         padded[8 + ROWS :, :] = jnp.zeros((8, LANES), F32)
         padded[8 : 8 + ROWS, :] = whole
         parts = [padded[4 + 16 * q : 4 + 16 * q + STRIP_ROWS, :].astype(BF16) for q in range(4)]
-        own = dot(jnp.concatenate(parts, axis=1), picks)
-        flat_halo[...] = jnp.zeros(flat_halo.shape, F32)
-        for q in range(4):
-            for g in range(max(0, 2 * q - 1), min(GROUPS, 2 * q + 3)):
-                start = 8 + 8 * g - 16 * q + EDGE_ROWS
-                flat_halo[start : start + 8, :] += strip_edges(edges[:RB], edges[RB:], f * GROUPS + g, q)
-        whole = (own + flat_halo[8 : 8 + STRIP_ROWS, :]) * gain
-        for row in range(STRIP_ROWS):
-            strip_ref[row * 8 : row * 8 + 8, :] = jnp.broadcast_to(whole[row : row + 1], (8, LANES))
+        flat_own[f] = dot(jnp.concatenate(parts, axis=1), picks)
+
+    settle(edge_recv, n_r.at[0])
+    merged = edge_recv[0].astype(F32) + edge_recv[1].astype(F32)
+    surface = jnp.zeros((RB, LANES), F32)
+    for f in range(FIELDS):
+        rows = slice((f + 2) * RB, (f + 3) * RB)
+        for side, s, shift in ((0, 2, 64 + 8 * f), (1, 0, 72 + 8 * f)):
+            moved = pltpu.roll(obs[s, rows, :].astype(F32), shift, 1)
+            surface = jnp.where(at_lane // HALO == 16 + 2 * f + side, moved, surface)
+    for to in range(GROUPS):
+        rows = slice(to * 8, to * 8 + 8)
+        send_e[to] = jnp.concatenate([merged[rows, :LANES], merged[rows, LANES:] + surface], axis=0).astype(BF16)
+    for step in far_first:
+        to, there = member_device(step)
+        if step:
+            remote(send_e.at[to], recv_e.at[z], e_s.at[0], e_r.at[0], there).start()
+        else:
+            send_or_keep(at_home, send_e.at[to], recv_e.at[z], e_s.at[0], e_r.at[0], there)
 
     def pressure(x):
         return 0.125 * (jnp.maximum(x, 0.0) + jnp.log1p(jnp.exp(-jnp.abs(x))))
@@ -439,34 +405,46 @@
                 parts = [final[v, pl.ds((start + h * 8) * 8 + j, 8, stride=8), :] for h in range(2)]
                 out[j, v, start : start + 16, :] = jnp.concatenate(parts, axis=0).astype(BF16)
 
+    strip_rows = STRIP_ROWS * 8
+
+    def strip_own(v):
+        parts = [recv_c[v, 128 * q : 128 * q + strip_rows, :] for q in range(4)]
+        return dot(jnp.concatenate(parts, axis=1), picks)
+
     unpack(0)
     write_out(0)
+    strip_halo[0] = strip_own(0)
     unpack(1)
+    strip_halo[1] = strip_own(1)
     settle(recv_e, e_r.at[0])
+    edges = [recv_e[g].astype(F32) for g in range(GROUPS)]
     for row in range(STRIP_ROWS):
         for v in range(FIELDS):
-            total = none
+            total = none if v == 2 else strip_halo[v, row * 8 : row * 8 + 8, :]
             for q in range(4):
                 at = 16 * q - EDGE_ROWS + row
                 if 0 <= at < ROWS:
-                    edges = recv_e[at // RB].astype(F32)
-                    total = total + strip_edges(edges[:8], edges[8:], v * RB + at % RB, q)
+                    j = v * RB + at % RB
+                    total = total + strip_edges(edges[at // RB][j // 16 * 8 : j // 16 * 8 + 8], j % 16, q)
             strip_halo[v, row * 8 : row * 8 + 8, :] = total
+    for f, (strip_ref, gain) in enumerate(((strip_free, 1.0 / 1.5), (strip_tau_x, 0.5), (strip_tau_y, 0.5))):
+        flat_halo[...] = jnp.zeros(flat_halo.shape, F32)
+        for q in range(4):
+            for g in range(max(0, 2 * q - 1), min(GROUPS, 2 * q + 3)):
+                start = 8 + 8 * g - 16 * q + EDGE_ROWS
+                flat_halo[start : start + 8, :] += strip_edges(edges[g][8:], 8 + f, q)
+        whole = (flat_own[f] + flat_halo[8 : 8 + STRIP_ROWS, :]) * gain
+        for row in range(STRIP_ROWS):
+            strip_ref[row * 8 : row * 8 + 8, :] = jnp.broadcast_to(whole[row : row + 1], (8, LANES))
+    row = iota((strip_rows, LANES), 0) // 8
+    group = iota((strip_rows, LANES), 1) // 32
+    outside = jnp.logical_or(
+        jnp.logical_and(group == 0, row < EDGE_ROWS), jnp.logical_and(group == 3, row >= STRIP_ROWS - EDGE_ROWS)
+    )
+    strip_press[...] = jnp.where(outside, 0.0, pressure(strip_halo[0]))
+    strip_x[8 : 8 + strip_rows, :] = strip_halo[1]
     unpack(2)
-
-    strip_rows = STRIP_ROWS * 8
-    for v in range(FIELDS):
-        parts = [recv_c[v, 128 * q : 128 * q + strip_rows, :] for q in range(4)]
-        strip = dot(jnp.concatenate(parts, axis=1), picks) + strip_halo[v]
-        if v == 0:
-            row = iota((strip_rows, LANES), 0) // 8
-            group = iota((strip_rows, LANES), 1) // 32
-            outside = jnp.logical_or(
-                jnp.logical_and(group == 0, row < EDGE_ROWS), jnp.logical_and(group == 3, row >= STRIP_ROWS - EDGE_ROWS)
-            )
-            strip_press[...] = jnp.where(outside, 0.0, pressure(strip))
-        else:
-            (strip_x, strip_y)[v - 1][8 : 8 + strip_rows, :] = strip
+    strip_y[8 : 8 + strip_rows, :] = strip_halo[2] + strip_own(2)
 
     def difference(x):
         return pltpu.roll(x, LANES - 1, 1) - pltpu.roll(x, 1, 1)
@@ -515,7 +493,7 @@
     settle(thick.at[pl.ds(0, 2)], b_s.at[0])
     settle(obs.at[pl.ds(0, 2)], b_s.at[1])
     settle(edge_send, n_s.at[0])
-    for sent, sem in ((thick.at[1], at_s), (drift, ad_s), (recv_e, e_s), (recv_w, w_s)):
+    for sent, sem in ((thick.at[1], at_s), (drift, ad_s), (recv_e, e_s)):
 
         @pl.when(at_home)
         def _():
@@ -563,20 +541,20 @@
             pltpu.VMEM((ENS, CELLS), BF16),
             pltpu.VMEM((16, CELLS), BF16),
             pltpu.VMEM((WIDE, CELLS), BF16),
+            pltpu.VMEM((WIDE, CELLS), BF16),
             pltpu.VMEM((ENS, WIDE), F32),
             pltpu.VMEM((PATCHES, ENS), F32),
             pltpu.VMEM((WIDE, FIELDS * RB * LANES), BF16),
-            pltpu.VMEM((2, ENS, LANES), F32),
-            pltpu.VMEM((2, ENS, LANES), BF16),
-            pltpu.VMEM((2, ENS, LANES), BF16),
+            pltpu.VMEM((2, 2, ENS, LANES), F32),
+            pltpu.VMEM((2, ENS, 2 * LANES), BF16),
+            pltpu.VMEM((2, ENS, 2 * LANES), BF16),
             pltpu.VMEM((FIELDS, GROUPS, 64, LANES), BF16),
             pltpu.VMEM((FIELDS, (ROWS + 2 * EDGE_ROWS) * 8, LANES), BF16),
             pltpu.VMEM((GROUPS, 16, LANES), BF16),
             pltpu.VMEM((GROUPS, 16, LANES), BF16),
             pltpu.VMEM((FIELDS, ROWS, LANES), F32),
-            pltpu.VMEM((16, LANES), BF16),
-            pltpu.VMEM((GROUPS, 16, LANES), BF16),
             pltpu.VMEM((ROWS + 16, LANES), F32),
+            pltpu.VMEM((FIELDS, STRIP_ROWS, LANES), F32),
             pltpu.VMEM((STRIP_ROWS + 16, LANES), F32),
             pltpu.VMEM((FIELDS, STRIP_ROWS * 8, LANES), F32),
             *[pltpu.VMEM((ROWS * 8, LANES), F32)] * 4,
@@ -591,7 +569,6 @@
             dma((2,)), dma((3, 2)),
             dma((1,)), dma((1,)),
             dma((1,)), dma((FIELDS,)),
-            dma((1,)), dma((1,)),
             dma((1,)), dma((1,)),
         ],
         compiler_params=pltpu.CompilerParams(

time: 42.5 us -> 42.2 us (level)
  no operation moved by 1% of the time
where the time goes in v4:
time: 42.2 us; the launch traced here: 42.1 us
  Pallas kernels  41.3 us (98%)
  local copies, waits for them, and re-layouts  0.75 us (2%)
    pallas_call x1, Pallas kernels, body(): pl.pallas_call(functools.partial(kernel, tiles), out_shape=jax.ShapeDtype...  41.3 us

profile of v4, /device:TPU:1, one launch (start us, length us, event | category | flops | bytes accessed | tf_op | source)
XLA Modules:
  0.0 42.1 jit_solution(13738272241100523012)
XLA Ops:
  0.0 41.3 %analysis_and_drift.1 = bf16[8,3,64,128]{3,2,1,0:T(8,128)(2,1)S(1)} custom-call(bf16[8,3,8,8,128]{4,3,2,1,0:T(8,128)(2,1)} %bitcast.2, bf16[8,128]{1,0:T(8,128)(2,1)} %obs_value_hbm.1, bf16[8,128]{1,0:T(8,128)(2,1)} %obs_var_hbm.1, s32[8,256]{1,0:T(8,128)} %bitcast.3, s32[64,128]{1,0:T(8,128)} %mask_hbm.1, bf16[2,64,128]{2,1,0:T(8,128)(2,1)} %wind_hbm.1), custom_call_target="tpu_custom_call" | custom-call | tf_op jit(solution)/shard_map/analysis_and_drift/pallas_call | solution.py:521
  41.3 0.7 %copy.8 = bf16[8,3,64,128]{3,2,1,0:T(8,128)(2,1)} copy(bf16[8,3,64,128]{3,2,1,0:T(8,128)(2,1)S(1)} %analysis_and_drift.1) | data formatting | bytes 786432

commit v5 on v4

--- a/solution.py
+++ b/solution.py
@@ -105,7 +105,7 @@
     out,
     obs_value, obs_var, ice_mask, wind,
     staged, tall, send_obs, thick, drift, obs, index,
-    count, weight, anom_hi, anom_lo, pulls, heavy, heavy_lo, acc, projected,
+    count, weight, anom_hi, anom_lo, pulls, heavy, acc, projected,
     masked, packed, edge_send, edge_recv,
     send_c, recv_c, send_e, recv_e,
     flat_rows, padded, flat_own, flat_halo, strip_halo,
@@ -261,13 +261,11 @@
                 pulls[:, lanes] = jnp.concatenate([pull_high, pull - pull_high], axis=0).astype(BF16)
                 for p in range(PATCHES):
                     row = p * RB + r
-                    high, low = split(anom * weight[row : row + 1, :])
-                    heavy[p * ENS : (p + 1) * ENS, lanes] = high
-                    heavy_lo[p * ENS : (p + 1) * ENS, lanes] = low
+                    heavy[p * ENS : (p + 1) * ENS, lanes] = (anom * weight[row : row + 1, :]).astype(BF16)
             at = (place * RB + pair * 2) * LANES
             span = slice(at, at + 2 * LANES)
             main = dot_lanes(jnp.concatenate([anom_hi[:, span], anom_lo[:, span]], axis=0), heavy[:, span])
-            part = main[:ENS] + main[ENS:] + dot_lanes(anom_hi[:, span], heavy_lo[:, span])
+            part = main[:ENS] + main[ENS:]
             drawn = dot_lanes(pulls[:, span], anom_hi[:, span]) + dot_lanes(pulls[:, span], anom_lo[:, span])
             drawn = drawn[:PATCHES] + drawn[PATCHES:]
             if place == 0 and pair == 0:
@@ -540,7 +538,6 @@
             pltpu.VMEM((ENS, CELLS), BF16),
             pltpu.VMEM((ENS, CELLS), BF16),
             pltpu.VMEM((16, CELLS), BF16),
-            pltpu.VMEM((WIDE, CELLS), BF16),
             pltpu.VMEM((WIDE, CELLS), BF16),
             pltpu.VMEM((ENS, WIDE), F32),
             pltpu.VMEM((PATCHES, ENS), F32),

time: 42.2 us -> 41.9 us (level)
  no operation moved by 1% of the time
where the time goes in v5:
time: 41.9 us; the launch traced here: 41.8 us
  Pallas kernels  41 us (98%)
  local copies, waits for them, and re-layouts  0.75 us (2%)
    pallas_call x1, Pallas kernels, body(): pl.pallas_call(functools.partial(kernel, tiles), out_shape=jax.ShapeDtype...  41 us

profile of v5, /device:TPU:1, one launch (start us, length us, event | category | flops | bytes accessed | tf_op | source)
XLA Modules:
  0.0 41.8 jit_solution(5739673355599834090)
XLA Ops:
  0.0 41.0 %analysis_and_drift.1 = bf16[8,3,64,128]{3,2,1,0:T(8,128)(2,1)S(1)} custom-call(bf16[8,3,8,8,128]{4,3,2,1,0:T(8,128)(2,1)} %bitcast.2, bf16[8,128]{1,0:T(8,128)(2,1)} %obs_value_hbm.1, bf16[8,128]{1,0:T(8,128)(2,1)} %obs_var_hbm.1, s32[8,256]{1,0:T(8,128)} %bitcast.3, s32[64,128]{1,0:T(8,128)} %mask_hbm.1, bf16[2,64,128]{2,1,0:T(8,128)(2,1)} %wind_hbm.1), custom_call_target="tpu_custom_call" | custom-call | tf_op jit(solution)/shard_map/analysis_and_drift/pallas_call | solution.py:519
  41.0 0.7 %copy.8 = bf16[8,3,64,128]{3,2,1,0:T(8,128)(2,1)} copy(bf16[8,3,64,128]{3,2,1,0:T(8,128)(2,1)S(1)} %analysis_and_drift.1) | data formatting | bytes 786432
